TPU v7x, 32 devices: a whole 2x2x4 slice. The times are simulated.
32 devices in a mesh: dp: 4 (over z), expert: 8 (over y, x, core).
Axes of the slice: x: 2, y: 2, z: 4, core: 2. Of those that a mesh axis runs over, the one named last changes fastest.
Arguments:
- tokens: bfloat16 [8192, 1536], P(('dp', 'expert')), may hold values from -6 to 6
- lengths: int32 [4, 4], P('dp'), may hold values from 1 to 1024, 2048 in all within a row
- seq_order: int32 [4, 4], P('dp'), may hold values from 0 to 3, each once within a row
- routes: int32 [8192, 4], P(('dp', 'expert')), may hold values from 0 to 7, all different within a row; in each aligned block of 256 rows (0 to 255, 256 to 511, ...) at most 256 rows name the same one
- norm_attn: bfloat16 [1536], P(('dp', 'expert')), may hold values from 0.5 to 1.5
- w_query: bfloat16 [1536, 1536], P(('dp', 'expert')), may hold values from -0.15625 to 0.15625
- key_projection: bfloat16 [1536, 256], P(('dp', 'expert')), may hold values from -0.15625 to 0.15625
- value_projection: bfloat16 [1536, 256], P(('dp', 'expert')), may hold values from -0.15625 to 0.15625
- w_out: bfloat16 [1536, 1536], P(('dp', 'expert')), may hold values from -1.25 to 1.25
- norm_moe: bfloat16 [1536], P(('dp', 'expert')), may hold values from 0.5 to 1.5
- w_router: bfloat16 [1536, 8], P(('dp', 'expert')), may hold values from -0.078125 to 0.078125
- w_gate: bfloat16 [8, 1536, 768], P('expert', 'dp'), may hold values from -0.15625 to 0.15625
- w_up: bfloat16 [8, 1536, 768], P('expert', 'dp'), may hold values from -0.15625 to 0.15625
- w_down: bfloat16 [8, 768, 1536], P('expert', 'dp'), may hold values from -0.21875 to 0.21875
- cotangent: bfloat16 [8192, 1536], P(('dp', 'expert')), may hold values from -6 to 6
Outputs:
- output: bfloat16 [8192, 1536], P(('dp', 'expert'))
- tokens_grad: bfloat16 [8192, 1536], P(('dp', 'expert'))
- norm_attn_grad: float32 [1536], P(('dp', 'expert'))
- w_query_grad: float32 [1536, 1536], P(('dp', 'expert'))
- w_key_grad: float32 [1536, 256], P(('dp', 'expert'))
- w_value_grad: float32 [1536, 256], P(('dp', 'expert'))
- w_out_grad: float32 [1536, 1536], P(('dp', 'expert'))
- norm_moe_grad: float32 [1536], P(('dp', 'expert'))
- w_router_grad: float32 [1536, 8], P(('dp', 'expert'))
- w_gate_grad: float32 [8, 1536, 768], P('expert', 'dp')
- w_up_grad: float32 [8, 1536, 768], P('expert', 'dp')
- w_down_grad: float32 [8, 768, 1536], P('expert', 'dp')
Inputs may be any that keep to these rules, and one draw needn't show every extreme that they name: In each group the lengths sum to 2048 and the largest is exactly 1024. `seq_order`: each row holds every number below 4 once. `routes`: each row names 4 different experts; among the rows of one device no expert is named more than 256 times, a bound that some block reaches.
All inputs are finite; a program needn't handle non-finite values.
Results may differ from a plain program's by a relative error of at most 0.018.
Values may be sent and summed in bfloat16 or wider, within the bound.
A program may use at most 256 MiB of HBM per device.

v0:
```python
import math

import jax
import jax.numpy as jnp
from jax import lax
from jax.sharding import PartitionSpec as P

QUERY_HEADS = 12
KEY_VALUE_HEADS = 2
HEAD_SIZE = 128


EPSILON = 1e-06
ROPE_BASE = 10000.0
MASKED_SCORE = -1e30


def rms_scale(values):
    return lax.rsqrt(jnp.mean(values * values, axis=-1, keepdims=True) + EPSILON)


def softmax_last(values):
    highest = jnp.max(values, axis=-1, keepdims=True)
    spread = jnp.exp(values - highest)
    return spread / jnp.sum(spread, axis=-1, keepdims=True)


def rope_tables(positions, half_size):
    angle_steps = lax.broadcasted_iota(jnp.float32, (half_size,), 0)
    frequency = jnp.exp(angle_steps * (-math.log(ROPE_BASE) / half_size))
    angles = positions.astype(jnp.float32)[:, None] * frequency
    return (jnp.cos(angles)[:, None, :], jnp.sin(angles)[:, None, :])


def apply_rotation(values, cosine_table, sine_table):
    half_size = values.shape[-1] // 2
    first = values[..., :half_size]
    second = values[..., half_size:]
    return jnp.concatenate(
        [first * cosine_table - second * sine_table, second * cosine_table + first * sine_table],
        axis=-1,
    )


def reverse_rotation(grads_in, cosine_table, sine_table):
    half_size = grads_in.shape[-1] // 2
    first = grads_in[..., :half_size]
    second = grads_in[..., half_size:]
    return jnp.concatenate(
        [first * cosine_table + second * sine_table, second * cosine_table - first * sine_table],
        axis=-1,
    )


def seq_layout(lengths, seq_order):
    count_seq = lengths.shape[1]
    picked = seq_order[0][:, None] == lax.broadcasted_iota(jnp.int32, (count_seq, count_seq), 1)
    ordered = jnp.sum(jnp.where(picked, lengths[0][None, :], 0), axis=1)
    return (ordered, jnp.cumsum(ordered))


def seq_place(positions, ordered, seq_ends):
    passed = seq_ends[None, :] <= positions[:, None]
    sequence_index = jnp.sum(passed.astype(jnp.int32), axis=1)
    starts = jnp.sum(jnp.where(passed, ordered[None, :], 0), axis=1)
    return (sequence_index, positions - starts)


def block_scores(
    query_rows, key_portion, query_seq, query_stream, key_seq, key_stream, score_scale
):
    raw_scores = (
        jnp.einsum("tkrd,skd->krts", query_rows, key_portion, preferred_element_type=jnp.float32)
        * score_scale
    )
    allowed = (query_seq[:, None] == key_seq[None, :]) & (
        key_stream[None, :] <= query_stream[:, None]
    )
    return jnp.where(allowed, raw_scores, MASKED_SCORE)


def norm_backward(grad_normed, unit_values, inv_scale, gain_float):
    scaled = grad_normed * gain_float
    gain_grad = jnp.sum(grad_normed * unit_values, axis=0)
    input_grad = inv_scale * (
        scaled - unit_values * jnp.mean(scaled * unit_values, axis=-1, keepdims=True)
    )
    return (gain_grad, input_grad)


def on_device(
    tokens,
    lengths,
    seq_order,
    routes,
    norm_attn,
    w_query,
    key_projection,
    value_projection,
    w_out,
    norm_moe,
    w_router,
    w_gate,
    w_up,
    w_down,
    cotangent,
):
    gain_one, query_w, key_w, value_w, out_w, gain_two, router_w = (
        lax.all_gather(norm_attn, ("dp", "expert"), axis=0, tiled=True),
        lax.all_gather(w_query, ("dp", "expert"), axis=0, tiled=True),
        lax.all_gather(key_projection, ("dp", "expert"), axis=0, tiled=True),
        lax.all_gather(value_projection, ("dp", "expert"), axis=0, tiled=True),
        lax.all_gather(w_out, ("dp", "expert"), axis=0, tiled=True),
        lax.all_gather(norm_moe, ("dp", "expert"), axis=0, tiled=True),
        lax.all_gather(w_router, ("dp", "expert"), axis=0, tiled=True),
    )
    gate_w, up_w, down_w = (
        lax.all_gather(w_gate, "dp", axis=1, tiled=True),
        lax.all_gather(w_up, "dp", axis=1, tiled=True),
        lax.all_gather(w_down, "dp", axis=1, tiled=True),
    )
    token_count, width = tokens.shape
    group_size = lax.axis_size("expert")
    my_index = lax.axis_index("expert")
    query_per_key_heads = QUERY_HEADS // KEY_VALUE_HEADS
    key_value_width = KEY_VALUE_HEADS * HEAD_SIZE
    score_scale = 1.0 / math.sqrt(HEAD_SIZE)
    group_tokens = token_count * group_size
    seq_lens, seq_ends = seq_layout(lengths, seq_order)
    my_stream = lax.broadcasted_iota(jnp.int32, (token_count,), 0) * group_size + my_index
    query_seq, query_rel = seq_place(my_stream, seq_lens, seq_ends)
    all_rows = lax.broadcasted_iota(jnp.int32, (group_tokens,), 0)
    key_stream = all_rows % token_count * group_size + all_rows // token_count
    key_seq = seq_place(key_stream, seq_lens, seq_ends)[0]
    block_row_count = math.gcd(group_tokens, 512)
    block_count = group_tokens // block_row_count
    cosine_table, sine_table = rope_tables(query_rel, HEAD_SIZE // 2)
    inputs_float = tokens.astype(jnp.float32)
    inv_one = rms_scale(inputs_float)
    unit_one = inputs_float * inv_one
    normed_one = (unit_one * gain_one.astype(jnp.float32)).astype(jnp.bfloat16)
    query_pre = jnp.dot(normed_one, query_w, preferred_element_type=jnp.float32)
    key_before_rotation = jnp.dot(normed_one, key_w, preferred_element_type=jnp.float32)
    value_projected = jnp.dot(normed_one, value_w, preferred_element_type=jnp.float32)
    rotated_queries = (
        apply_rotation(
            query_pre.reshape(token_count, QUERY_HEADS, HEAD_SIZE), cosine_table, sine_table
        )
        .astype(jnp.bfloat16)
        .reshape(token_count, KEY_VALUE_HEADS, query_per_key_heads, HEAD_SIZE)
    )
    rotated_keys = apply_rotation(
        key_before_rotation.reshape(token_count, KEY_VALUE_HEADS, HEAD_SIZE),
        cosine_table,
        sine_table,
    ).astype(jnp.bfloat16)
    key_value = jnp.concatenate(
        [rotated_keys.reshape(token_count, key_value_width), value_projected.astype(jnp.bfloat16)],
        axis=1,
    )
    gathered = lax.all_gather(key_value, "expert", axis=0, tiled=True)
    key_blocks = (
        gathered.reshape(block_count, block_row_count, 2 * key_value_width),
        key_seq.reshape(block_count, block_row_count),
        key_stream.reshape(block_count, block_row_count),
    )

    def stats_step(carry, blocks):
        run_max, run_sum = carry
        key_value_block, seq_block, stream_block = blocks
        key_portion = key_value_block[:, :key_value_width].reshape(-1, KEY_VALUE_HEADS, HEAD_SIZE)
        scores = block_scores(
            rotated_queries, key_portion, query_seq, my_stream, seq_block, stream_block, score_scale
        )
        new_max = jnp.maximum(run_max, jnp.max(scores, axis=-1))
        run_sum = run_sum * jnp.exp(run_max - new_max) + jnp.sum(
            jnp.exp(scores - new_max[..., None]), axis=-1
        )
        return ((new_max, run_sum), None)

    initial_maximum = jnp.full(
        (KEY_VALUE_HEADS, query_per_key_heads, token_count), MASKED_SCORE, jnp.float32
    )
    (row_max, row_sum), unused = lax.scan(
        stats_step, (initial_maximum, jnp.zeros_like(initial_maximum)), key_blocks
    )
    log_total = row_max + jnp.log(row_sum)

    def value_step(carry, blocks):
        summed, residue = carry
        key_value_block, seq_block, stream_block = blocks
        key_portion = key_value_block[:, :key_value_width].reshape(-1, KEY_VALUE_HEADS, HEAD_SIZE)
        value_portion = key_value_block[:, key_value_width:].reshape(-1, KEY_VALUE_HEADS, HEAD_SIZE)
        scores = block_scores(
            rotated_queries, key_portion, query_seq, my_stream, seq_block, stream_block, score_scale
        )
        chances = jnp.exp(scores - log_total[..., None])
        low_chances = chances.astype(jnp.bfloat16)
        remainder = (chances - low_chances.astype(jnp.float32)).astype(jnp.bfloat16)
        summed = summed + jnp.einsum(
            "krts,skd->tkrd", low_chances, value_portion, preferred_element_type=jnp.float32
        )
        residue = residue + jnp.einsum(
            "krts,skd->tkrd", remainder, value_portion, preferred_element_type=jnp.float32
        )
        return ((summed, residue), None)

    empty_head_state = jnp.zeros(
        (token_count, KEY_VALUE_HEADS, query_per_key_heads, HEAD_SIZE), jnp.float32
    )
    (summed, residue), unused = lax.scan(
        value_step, (empty_head_state, empty_head_state), key_blocks
    )
    attended_full = summed + residue
    attended_low = summed.reshape(token_count, QUERY_HEADS * HEAD_SIZE).astype(jnp.bfloat16)
    middle = inputs_float + jnp.dot(attended_low, out_w, preferred_element_type=jnp.float32)
    inv_two = rms_scale(middle)
    unit_two = middle * inv_two
    normed_two = (unit_two * gain_two.astype(jnp.float32)).astype(jnp.bfloat16)
    logits = jnp.dot(normed_two, router_w, preferred_element_type=jnp.float32)
    n_experts = logits.shape[1]
    top_count = routes.shape[1]
    capacity = 2 * token_count * top_count // n_experts
    choose = routes[:, :, None] == lax.broadcasted_iota(jnp.int32, (1, 1, n_experts), 2)
    gates = softmax_last(jnp.sum(jnp.where(choose, logits[:, None, :], 0.0), axis=-1))
    flat_routes = routes.reshape(-1)
    flat_count = token_count * top_count
    one_hot = (flat_routes[:, None] == lax.broadcasted_iota(jnp.int32, (1, n_experts), 1)).astype(
        jnp.int32
    )
    places = jnp.sum((jnp.cumsum(one_hot, axis=0) - one_hot) * one_hot, axis=1)
    slot_ids = flat_routes * capacity + places
    matches = slot_ids[None, :] == lax.broadcasted_iota(jnp.int32, (n_experts * capacity, 1), 0)
    source = jnp.max(
        jnp.where(matches, lax.broadcasted_iota(jnp.int32, (1, flat_count), 1), -1), axis=1
    )
    filled = source >= 0
    source_row = jnp.maximum(source, 0)
    outgoing = jnp.where(
        filled[:, None], normed_two[source_row // top_count], jnp.zeros((), jnp.bfloat16)
    ).reshape(n_experts, capacity, width)
    local_experts = gate_w.shape[0]
    arrived = lax.all_to_all(outgoing, "expert", split_axis=0, concat_axis=0, tiled=True)
    item_count = arrived.shape[1]
    grouped = arrived.reshape(group_size, local_experts, item_count, width)
    gate_pre = jnp.einsum("sicd,idf->sicf", grouped, gate_w, preferred_element_type=jnp.float32)
    up_pre = jnp.einsum("sicd,idf->sicf", grouped, up_w, preferred_element_type=jnp.float32)
    hidden = (gate_pre * jax.nn.sigmoid(gate_pre) * up_pre).astype(jnp.bfloat16)
    produced = jnp.einsum(
        "sicf,ifd->sicd", hidden, down_w, preferred_element_type=jnp.float32
    ).astype(jnp.bfloat16)
    returned = lax.all_to_all(
        produced.reshape(group_size * local_experts, item_count, width),
        "expert",
        split_axis=0,
        concat_axis=0,
        tiled=True,
    )
    flat_shape = (group_size * local_experts, item_count, -1)
    returned, arrived, gate_pre, up_pre, hidden = (
        returned,
        arrived,
        gate_pre.reshape(flat_shape),
        up_pre.reshape(flat_shape),
        hidden.reshape(flat_shape),
    )
    back_rows = (
        returned.reshape(n_experts * capacity, width)[slot_ids]
        .reshape(token_count, top_count, width)
        .astype(jnp.float32)
    )
    output = (middle + jnp.sum(gates[:, :, None] * back_rows, axis=1)).astype(jnp.bfloat16)
    gain_one, query_w, key_w, value_w, out_w, gain_two, router_w = (
        lax.all_gather(norm_attn, ("dp", "expert"), axis=0, tiled=True),
        lax.all_gather(w_query, ("dp", "expert"), axis=0, tiled=True),
        lax.all_gather(key_projection, ("dp", "expert"), axis=0, tiled=True),
        lax.all_gather(value_projection, ("dp", "expert"), axis=0, tiled=True),
        lax.all_gather(w_out, ("dp", "expert"), axis=0, tiled=True),
        lax.all_gather(norm_moe, ("dp", "expert"), axis=0, tiled=True),
        lax.all_gather(w_router, ("dp", "expert"), axis=0, tiled=True),
    )
    gate_w, up_w, down_w = (
        lax.all_gather(w_gate, "dp", axis=1, tiled=True),
        lax.all_gather(w_up, "dp", axis=1, tiled=True),
        lax.all_gather(w_down, "dp", axis=1, tiled=True),
    )
    grad_out = cotangent.astype(jnp.float32)
    grad_gates = jnp.sum(grad_out[:, None, :] * back_rows, axis=-1)
    grad_chosen = gates * (grad_gates - jnp.sum(gates * grad_gates, axis=-1, keepdims=True))
    grad_logits = jnp.sum(jnp.where(choose, grad_chosen[:, :, None], 0.0), axis=1).astype(
        jnp.bfloat16
    )
    router_grad = jnp.einsum(
        "td,te->de", normed_two, grad_logits, preferred_element_type=jnp.float32
    )
    grad_normed_two = jnp.einsum(
        "te,de->td", grad_logits, router_w, preferred_element_type=jnp.float32
    )
    grad_returned = (
        (gates[:, :, None] * grad_out[:, None, :]).astype(jnp.bfloat16).reshape(flat_count, width)
    )
    grad_outgoing = jnp.where(
        filled[:, None], grad_returned[source_row], jnp.zeros((), jnp.bfloat16)
    ).reshape(n_experts, capacity, width)
    grad_produced = lax.all_to_all(grad_outgoing, "expert", split_axis=0, concat_axis=0, tiled=True)
    four_shape = (group_size, local_experts, capacity, -1)
    grad_prod = grad_produced.reshape(four_shape)
    gate_four = gate_pre.reshape(four_shape)
    up_four = up_pre.reshape(four_shape)
    arrived_four = arrived.reshape(four_shape)
    sigmoid_gate = jax.nn.sigmoid(gate_four)
    grad_hidden = jnp.einsum(
        "sicd,ifd->sicf", grad_prod, down_w, preferred_element_type=jnp.float32
    )
    down_grad = jnp.einsum(
        "sicf,sicd->ifd", hidden.reshape(four_shape), grad_prod, preferred_element_type=jnp.float32
    )
    grad_gate_pre = (
        grad_hidden * up_four * sigmoid_gate * (1.0 + gate_four * (1.0 - sigmoid_gate))
    ).astype(jnp.bfloat16)
    grad_up_pre = (grad_hidden * (gate_four * sigmoid_gate)).astype(jnp.bfloat16)
    gate_grad = jnp.einsum(
        "sicd,sicf->idf", arrived_four, grad_gate_pre, preferred_element_type=jnp.float32
    )
    up_grad = jnp.einsum(
        "sicd,sicf->idf", arrived_four, grad_up_pre, preferred_element_type=jnp.float32
    )
    grad_arrived = jnp.einsum(
        "sicf,idf->sicd", grad_gate_pre, gate_w, preferred_element_type=jnp.float32
    )
    grad_arrived = (
        grad_arrived
        + jnp.einsum("sicf,idf->sicd", grad_up_pre, up_w, preferred_element_type=jnp.float32)
    ).astype(jnp.bfloat16)
    grad_back = lax.all_to_all(
        grad_arrived.reshape(group_size * local_experts, capacity, width),
        "expert",
        split_axis=0,
        concat_axis=0,
        tiled=True,
    )
    grad_normed_two = grad_normed_two + jnp.sum(
        grad_back.reshape(n_experts * capacity, width)[slot_ids]
        .reshape(token_count, top_count, width)
        .astype(jnp.float32),
        axis=1,
    )
    gain_two_grad, grad_middle = norm_backward(
        grad_normed_two, unit_two, inv_two, gain_two.astype(jnp.float32)
    )
    grad_middle = grad_out + grad_middle
    grad_mixed = grad_middle.astype(jnp.bfloat16)
    out_grad = jnp.einsum("tc,td->cd", attended_low, grad_mixed, preferred_element_type=jnp.float32)
    attention_output_gradient = jnp.einsum(
        "td,cd->tc", grad_mixed, out_w, preferred_element_type=jnp.float32
    ).astype(jnp.bfloat16)
    head_gradient = attention_output_gradient.reshape(
        token_count, KEY_VALUE_HEADS, query_per_key_heads, HEAD_SIZE
    )
    row_dot = jnp.transpose(
        jnp.sum(head_gradient.astype(jnp.float32) * attended_full, axis=-1), (1, 2, 0)
    )

    def grad_step(query_grad, blocks):
        key_value_block, seq_block, stream_block = blocks
        key_portion = key_value_block[:, :key_value_width].reshape(-1, KEY_VALUE_HEADS, HEAD_SIZE)
        value_portion = key_value_block[:, key_value_width:].reshape(-1, KEY_VALUE_HEADS, HEAD_SIZE)
        scores = block_scores(
            rotated_queries, key_portion, query_seq, my_stream, seq_block, stream_block, score_scale
        )
        chances = jnp.exp(scores - log_total[..., None])
        low_chances = chances.astype(jnp.bfloat16)
        grad_chances = jnp.einsum(
            "tkrd,skd->krts", head_gradient, value_portion, preferred_element_type=jnp.float32
        )
        grad_scores = (chances * (grad_chances - row_dot[..., None])).astype(jnp.bfloat16)
        query_grad = query_grad + jnp.einsum(
            "krts,skd->tkrd", grad_scores, key_portion, preferred_element_type=jnp.float32
        )
        key_terms = (
            jnp.einsum(
                "krts,tkrd->skd", grad_scores, rotated_queries, preferred_element_type=jnp.float32
            )
            * score_scale
        )
        value_terms = jnp.einsum(
            "krts,tkrd->skd", low_chances, head_gradient, preferred_element_type=jnp.float32
        )
        return (query_grad, (key_terms, value_terms))

    query_grad, (key_terms, value_terms) = lax.scan(grad_step, empty_head_state, key_blocks)
    query_grad = query_grad * score_scale
    local_key_weight, value_mine = (
        lax.psum_scatter(
            key_terms.reshape(group_tokens, key_value_width).astype(jnp.bfloat16),
            "expert",
            scatter_dimension=0,
            tiled=True,
        ).astype(jnp.float32),
        lax.psum_scatter(
            value_terms.reshape(group_tokens, key_value_width).astype(jnp.bfloat16),
            "expert",
            scatter_dimension=0,
            tiled=True,
        ).astype(jnp.float32),
    )
    grad_query_pre = (
        reverse_rotation(
            query_grad.reshape(token_count, QUERY_HEADS, HEAD_SIZE), cosine_table, sine_table
        )
        .reshape(token_count, QUERY_HEADS * HEAD_SIZE)
        .astype(jnp.bfloat16)
    )
    grad_key_pre = (
        reverse_rotation(
            local_key_weight.reshape(token_count, KEY_VALUE_HEADS, HEAD_SIZE),
            cosine_table,
            sine_table,
        )
        .reshape(token_count, key_value_width)
        .astype(jnp.bfloat16)
    )
    grad_value_pre = value_mine.astype(jnp.bfloat16)
    grad_normed_one = jnp.einsum(
        "tc,dc->td", grad_query_pre, query_w, preferred_element_type=jnp.float32
    )
    grad_normed_one = grad_normed_one + jnp.einsum(
        "tc,dc->td", grad_key_pre, key_w, preferred_element_type=jnp.float32
    )
    grad_normed_one = grad_normed_one + jnp.einsum(
        "tc,dc->td", grad_value_pre, value_w, preferred_element_type=jnp.float32
    )
    query_w_grad = jnp.einsum(
        "td,tc->dc", normed_one, grad_query_pre, preferred_element_type=jnp.float32
    )
    key_w_grad = jnp.einsum(
        "td,tc->dc", normed_one, grad_key_pre, preferred_element_type=jnp.float32
    )
    value_w_grad = jnp.einsum(
        "td,tc->dc", normed_one, grad_value_pre, preferred_element_type=jnp.float32
    )
    gain_one_grad, grad_input = norm_backward(
        grad_normed_one, unit_one, inv_one, gain_one.astype(jnp.float32)
    )
    tokens_grad = (grad_middle + grad_input).astype(jnp.bfloat16)
    gain_one_mine, query_mine, key_w_mine, value_w_mine, out_mine, gain_two_mine, router_mine = (
        lax.psum_scatter(gain_one_grad, ("dp", "expert"), scatter_dimension=0, tiled=True),
        lax.psum_scatter(query_w_grad, ("dp", "expert"), scatter_dimension=0, tiled=True),
        lax.psum_scatter(key_w_grad, ("dp", "expert"), scatter_dimension=0, tiled=True),
        lax.psum_scatter(value_w_grad, ("dp", "expert"), scatter_dimension=0, tiled=True),
        lax.psum_scatter(out_grad, ("dp", "expert"), scatter_dimension=0, tiled=True),
        lax.psum_scatter(gain_two_grad, ("dp", "expert"), scatter_dimension=0, tiled=True),
        lax.psum_scatter(router_grad, ("dp", "expert"), scatter_dimension=0, tiled=True),
    )
    gate_mine, up_mine, down_mine = (
        lax.psum_scatter(
            gate_grad.astype(jnp.bfloat16), "dp", scatter_dimension=1, tiled=True
        ).astype(jnp.float32),
        lax.psum_scatter(
            up_grad.astype(jnp.bfloat16), "dp", scatter_dimension=1, tiled=True
        ).astype(jnp.float32),
        lax.psum_scatter(
            down_grad.astype(jnp.bfloat16), "dp", scatter_dimension=1, tiled=True
        ).astype(jnp.float32),
    )
    return (
        output,
        tokens_grad,
        gain_one_mine,
        query_mine,
        key_w_mine,
        value_w_mine,
        out_mine,
        gain_two_mine,
        router_mine,
        gate_mine,
        up_mine,
        down_mine,
    )


def solution(mesh):
    return jax.shard_map(
        on_device,
        mesh=mesh,
        in_specs=(
            P(("dp", "expert"), None),
            P("dp", None),
            P("dp", None),
            P(("dp", "expert"), None),
            P(("dp", "expert")),
            P(("dp", "expert"), None),
            P(("dp", "expert"), None),
            P(("dp", "expert"), None),
            P(("dp", "expert"), None),
            P(("dp", "expert")),
            P(("dp", "expert"), None),
            P("expert", "dp", None),
            P("expert", "dp", None),
            P("expert", "dp", None),
            P(("dp", "expert"), None),
        ),
        out_specs=(
            P(("dp", "expert"), None),
            P(("dp", "expert"), None),
            P(("dp", "expert")),
            P(("dp", "expert"), None),
            P(("dp", "expert"), None),
            P(("dp", "expert"), None),
            P(("dp", "expert"), None),
            P(("dp", "expert")),
            P(("dp", "expert"), None),
            P("expert", "dp", None),
            P("expert", "dp", None),
            P("expert", "dp", None),
        ),
        check_vma=False,
    )
```

profile of v0, /device:TPU:0, one launch (start us, length us, event | category | flops | bytes accessed | tf_op | source)
XLA Modules:
  0.0 1648.4 jit_solution(9951485414050102549)
XLA Ops:
  9.9 42.1 %all-reduce.5 = (bf16[1536]{0:T(1024)(128)(2,1)S(1)}, bf16[1536]{0:T(1024)(128)(2,1)S(1)}) all-reduce(bf16[1536]{0:T(1024)(128)(2,1)S(1)} %dynamic-update-slice, bf16[1536]{0:T(1024)(128)(2,1)S(1)} %dynamic-update-slice.1), channel_id=1, replica_groups=mesh['dp'=4,'expert'=8] {'dp','expert'}, use_global_device_ids=true, to_apply=%add | all-reduce | flops 3072 | bytes 12288
  53.4 42.7 %all_gather.44 = bf16[1536,256]{1,0:T(8,128)(2,1)S(1)} all-gather(bf16[48,256]{1,0:T(8,128)(2,1)} %param.27), channel_id=1, replica_groups=mesh['dp'=4,'expert'=8] {'dp','expert'}, dimensions={0}, use_global_device_ids=true | all-gather | bytes 811008 | tf_op jit(solution)/shard_map/all_gather | solution.py:111
  97.3 39.1 %all_gather.45 = bf16[1536,256]{1,0:T(8,128)(2,1)S(1)} all-gather(bf16[48,256]{1,0:T(8,128)(2,1)} %param.28), channel_id=1, replica_groups=mesh['dp'=4,'expert'=8] {'dp','expert'}, dimensions={0}, use_global_device_ids=true | all-gather | bytes 811008 | tf_op jit(solution)/shard_map/all_gather | solution.py:112
  146.3 38.2 %all-gather = bf16[32,48,8]{1,2,0:T(8,128)(2,1)S(1)} all-gather(bf16[1,48,8]{1,2,0:T(8,128)(2,1)S(1)} %bitcast.454), channel_id=1, replica_groups=mesh['dp'=4,'expert'=8] {'dp','expert'}, dimensions={0}, use_global_device_ids=true | all-gather | bytes 25344 | tf_op jit(solution)/shard_map/all_gather | solution.py:115
  188.1 7.9 mul.436
  197.9 34.6 %all-gather.10.cloned.1.call-done = bf16[1536,1536]{1,0:T(8,128)(2,1)} async-done(((bf16[48,1536]{1,0:T(8,128)(2,1)}), bf16[1536,1536]{1,0:T(8,128)(2,1)}) %all-gather.10.cloned.1.call-update) | async-done | bytes 4718608 | tf_op jit(solution)/shard_map/all_gather | solution.py:110
  232.5 4.3 fusion.118
  241.2 33.0 %while.41 = (s32[]{:T(128)}, f32[2,6,256]{2,1,0:T(8,128)S(1)}, f32[2,6,256]{2,1,0:T(8,128)S(1)}, s32[256]{0:T(256)S(1)}, s32[4,512]{1,0:T(4,128)S(1)}, /*index=5...) while((s32[]{:T(128)}, f32[2,6,256]{2,1,0:T(8,128)S(1)}, ...), condition=%wide.region_9.10_spmd.clone, body=%wide.region_6.9_spmd.clone.sunk | while | flops 414072320 | bytes 15772804 | solution.py:184
  245.4 4.1 exponential_reduce_fusion.2
  253.6 4.1 exponential_reduce_fusion.2
  261.9 4.1 exponential_reduce_fusion.2
  266.3 3.8 fusion.207
  270.1 4.1 exponential_reduce_fusion.2
  274.3 57.8 %while.42 = (s32[]{:T(128)}, f32[256,2,6,128]{0,3,2,1:T(8,128)}, f32[256,2,6,128]{0,3,2,1:T(8,128)}, bf16[4,512,512]{1,2,0:T(8,128)(2,1)S(1)}, s32[256]{0:T(256)...) while((s32[]{:T(128)}, f32[256,2,6,128]{0,3,2,1:T(8,128)}, ...), condition=%wide.region_11.12_spmd.clone, body=%wide.region_10.11_spmd.clone.sunk | while | flops 1227227648 | bytes 54434980 | solution.py:211
  278.3 6.0 bitcast_add_fusion.7
  291.3 6.4 bitcast_add_fusion.7
  297.8 4.4 bitcast_add_fusion.6
  306.2 6.4 bitcast_add_fusion.7
  312.6 4.4 bitcast_add_fusion.6
  321.0 6.4 bitcast_add_fusion.7
  327.4 4.4 bitcast_add_fusion.6
  335.5 4.3 multiply_reduce_fusion.5
  341.9 10.2 gather_fusion
  352.1 4.8 multiply_convert_fusion
  357.0 15.6 gather_fusion.2
  372.6 10.0 broadcast_select_fusion
  382.6 4.8 all-to-all-start.2
  388.5 70.4 %all-to-all-done.2 = bf16[8,256,1536]{2,1,0:T(8,128)(2,1)} async-done(((bf16[8,256,1536]{2,1,0:T(8,128)(2,1)}), bf16[8,256,1536]{2,1,0:T(8,128)(2,1)}, u32[]{:S(2)}, u32[]{:S(2)}) %all-to-all-start.2) | async-done | bytes 6291488 | tf_op jit(solution)/shard_map/all_to_all | solution.py:305
  458.9 4.8 all-to-all-start
  464.3 9.6 fusion.67
  473.9 16.4 all-gather.16.cloned.1.call-done
  490.4 45.0 %all-to-all-done = bf16[8,256,1536]{2,1,0:T(8,128)(2,1)} async-done(((bf16[8,256,1536]{2,1,0:T(8,128)(2,1)}), bf16[8,256,1536]{2,1,0:T(8,128)(2,1)}, u32[]{:S(2)}, u32[]{:S(2)}) %all-to-all-start) | async-done | bytes 6291488 | tf_op jit(solution)/shard_map/all_to_all | solution.py:243
  535.3 9.6 fusion.71
  544.9 13.5 fusion.54
  560.1 6.9 convolution_convert_fusion
  567.0 5.2 all-to-all-start.1
  572.3 8.2 fusion.56
  580.5 7.4 add_convert_fusion
  587.9 55.9 %all-to-all-done.1 = bf16[8,256,1536]{2,1,0:T(8,128)(2,1)} async-done(((bf16[8,256,1536]{2,1,0:T(8,128)(2,1)}), bf16[8,256,1536]{2,1,0:T(8,128)(2,1)}, u32[]{:S(2)}, u32[]{:S(2)}) %all-to-all-start.1) | async-done | bytes 6291488 | tf_op jit(solution)/shard_map/all_to_all | solution.py:252
  643.9 4.8 all-to-all-start.3
  650.6 10.9 gather_fusion.1
  661.5 6.7 reshape.556
  668.2 9.6 multiply_reduce_fusion
  677.9 42.3 %all-to-all-done.3 = bf16[8,256,1536]{2,1,0:T(8,128)(2,1)} async-done(((bf16[8,256,1536]{2,1,0:T(8,128)(2,1)}), bf16[8,256,1536]{2,1,0:T(8,128)(2,1)}, u32[]{:S(2)}, u32[]{:S(2)}) %all-to-all-start.3) | async-done | bytes 6291488 | tf_op jit(solution)/shard_map/all_to_all | solution.py:335
  720.3 10.9 gather_fusion.3
  731.1 6.8 reshape.557
  738.0 7.7 reduce_sum.196
  760.7 65.4 %while.43 = (s32[]{:T(128)}, f32[256,2,6,128]{0,3,2,1:T(8,128)S(1)}, bf16[4,512,2,128]{3,1,2,0:T(8,128)(2,1)}, bf16[4,512,2,128]{3,1,2,0:T(8,128)(2,1)}, bf16[4,...) while((s32[]{:T(128)}, ...), condition=%wide.region_28.29_spmd.clone, body=%wide.region_27.28_spmd.clone.sunk | while | flops 2030305792 | bytes 105189736 | solution.py:391
  833.0 9.3 fusion.58
  842.4 9.7 fusion.61
  852.2 9.4 fusion.62
  867.2 36.7 %reduce-scatter.15.cloned.1.call-done = bf16[256,256]{1,0:T(8,128)(2,1)} async-done(((bf16[2048,256]{1,0:T(8,128)(2,1)}), bf16[256,256]{1,0:T(8,128)(2,1)}) %reduce-scatter.15.cloned.1.call-update) | async-done | bytes 131088 | tf_op jit(solution)/shard_map/reduce_scatter | solution.py:400
  906.6 6.5 fusion.84
  913.7 5.2 fusion.116
  919.0 35.1 %reduce-scatter.25.cloned.1.call-done = bf16[1,384,768]{2,1,0:T(8,128)(2,1)} async-done(((bf16[1,1536,768]{2,1,0:T(8,128)(2,1)}), bf16[1,384,768]{2,1,0:T(8,128)(2,1)}) %reduce-scatter.25.cloned.1.call-update) | async-done | bytes 589840 | tf_op jit(solution)/shard_map/reduce_scatter | solution.py:456
  956.2 47.7 %reduce-scatter.27.cloned.1.call-done = bf16[1,384,768]{2,1,0:T(8,128)(2,1)} async-done(((bf16[1,1536,768]{2,1,0:T(8,128)(2,1)}), bf16[1,384,768]{2,1,0:T(8,128)(2,1)}) %reduce-scatter.27.cloned.1.call-update) | async-done | bytes 589840 | tf_op jit(solution)/shard_map/reduce_scatter | solution.py:459
  1006.1 47.7 %reduce-scatter.29.cloned.1.call-done = bf16[1,192,1536]{2,1,0:T(8,128)(2,1)} async-done(((bf16[1,768,1536]{2,1,0:T(8,128)(2,1)}), bf16[1,192,1536]{2,1,0:T(8,128)(2,1)}) %reduce-scatter.29.cloned.1.call-update) | async-done | bytes 589840 | tf_op jit(solution)/shard_map/reduce_scatter | solution.py:462
  1056.0 5.1 fusion.130
  1061.1 92.9 %reduce-scatter.31.cloned.1.call-done = f32[48,8]{1,0:T(8,128)} async-done(((f32[1536,8]{1,0:T(8,128)}), f32[48,8]{1,0:T(8,128)}) %reduce-scatter.31.cloned.1.call-update) | async-done | bytes 1552
  1159.0 40.1 %all-reduce.4 = (f32[1536]{0:T(1024)S(1)}, f32[1536]{0:T(1024)S(1)}) all-reduce(f32[1536]{0:T(1024)S(1)} %get-tuple-element.467, f32[1536]{0:T(1024)S(1)} %copy-done.39), channel_id=4, replica_groups=mesh['dp'=4,'expert'=8] {'dp','expert'}, use_global_device_ids=true, to_apply=%region_33.34.clone | all-reduce | flops 3072 | bytes 24576
  1203.0 52.7 %reduce-scatter.19.cloned.1.call-done = f32[48,256]{1,0:T(8,128)} async-done(((f32[1536,256]{1,0:T(8,128)}), f32[48,256]{1,0:T(8,128)}) %reduce-scatter.19.cloned.1.call-update) | async-done | bytes 49168 | tf_op jit(solution)/shard_map/reduce_scatter | solution.py:449
  1255.7 102.0 %reduce-scatter.21.cloned.1.call-done = f32[48,256]{1,0:T(8,128)} async-done(((f32[1536,256]{1,0:T(8,128)}), f32[48,256]{1,0:T(8,128)}) %reduce-scatter.21.cloned.1.call-update) | async-done | bytes 49168 | tf_op jit(solution)/shard_map/reduce_scatter | solution.py:450
  1357.7 141.0 %reduce-scatter.23.cloned.1.call-done = f32[48,1536]{1,0:T(8,128)} async-done(((f32[1536,1536]{1,0:T(8,128)}), f32[48,1536]{1,0:T(8,128)}) %reduce-scatter.23.cloned.1.call-update) | async-done | bytes 294928 | tf_op jit(solution)/shard_map/reduce_scatter | solution.py:451
  1498.7 142.1 %reduce-scatter.17.cloned.1.call-done = f32[48,1536]{1,0:T(8,128)} async-done(((f32[1536,1536]{1,0:T(8,128)}), f32[48,1536]{1,0:T(8,128)}) %reduce-scatter.17.cloned.1.call-update) | async-done | bytes 294928 | tf_op jit(solution)/shard_map/reduce_scatter | solution.py:448
  (394 shorter events, 177.3 us)
Async XLA Ops:
  8.0 130.4 %copy-start.9 = (bf16[256,1536]{1,0:T(8,128)(2,1)S(1)}, bf16[256,1536]{1,0:T(8,128)(2,1)}, u32[]{:S(2)}) copy-start(bf16[256,1536]{1,0:T(8,128)(2,1)} %param.21) | copy-start | bytes 2359300
  8.0 188.1 %all-gather.8.cloned.1.call-start = ((), (), s32[]{:S(2)}) async-start(), calls=%async_computation.14 | async-start | bytes 2359296 | tf_op jit(solution)/shard_map/all_gather | solution.py:161
  52.0 180.5 %copy-start.28 = (f32[1536]{0:T(1024)}, f32[1536]{0:T(1024)S(1)}, u32[]{:S(2)}) copy-start(f32[1536]{0:T(1024)S(1)} %convert_element_type.181) | copy-start | bytes 18436
  53.4 179.1 %copy-start.35 = (f32[256]{0:T(256)}, f32[256]{0:T(256)S(1)}, u32[]{:S(2)}) copy-start(f32[256]{0:T(256)S(1)} %add_rsqrt_fusion.1) | copy-start | bytes 3076
  96.1 40.3 %copy-start.18 = (bf16[1536,256]{1,0:T(8,128)(2,1)}, bf16[1536,256]{1,0:T(8,128)(2,1)S(1)}, u32[]{:S(2)}) copy-start(bf16[1536,256]{1,0:T(8,128)(2,1)S(1)} %all_gather.44) | copy-start | bytes 2359300
  136.4 5.3 copy-start.34
  136.4 9.9 copy-start.44
  138.4 46.2 %copy-start.16 = (bf16[256,1536]{1,0:T(8,128)(2,1)S(1)}, bf16[256,1536]{1,0:T(8,128)(2,1)}, u32[]{:S(2)}) copy-start(bf16[256,1536]{1,0:T(8,128)(2,1)} %param.35) | copy-start | bytes 2359300
  139.3 97.6 %copy-start.22 = (f32[256,64]{0,1:T(8,128)}, f32[256,64]{0,1:T(8,128)S(1)}, u32[]{:S(2)}) copy-start(f32[256,64]{0,1:T(8,128)S(1)} %get-tuple-element.570) | copy-start | bytes 196612
  139.3 97.6 %copy-start.24 = (f32[256,64]{0,1:T(8,128)}, f32[256,64]{0,1:T(8,128)S(1)}, u32[]{:S(2)}) copy-start(f32[256,64]{0,1:T(8,128)S(1)} %get-tuple-element.571) | copy-start | bytes 196612
  140.1 92.4 %all-gather.10.cloned.1.call-start = ((), (), s32[]{:S(2)}) async-start(), calls=%async_computation.15 | async-start | bytes 4866048 | tf_op jit(solution)/shard_map/all_gather | solution.py:110
  140.9 194.7 %all-gather.12.cloned.1.call-start = ((), (), s32[]{:S(2)}) async-start(), calls=%async_computation.16 | async-start | bytes 4866048 | tf_op jit(solution)/shard_map/all_gather | solution.py:113
  144.9 43.2 %copy-start.37 = (s32[1024]{0:T(1024)}, s32[1024]{0:T(1024)S(1)}, u32[]{:S(2)}) copy-start(s32[1024]{0:T(1024)S(1)} %fusion.89) | copy-start | bytes 12292
  278.3 6.0 copy-start.7
  291.3 6.4 copy-start.7
  306.2 6.4 copy-start.7
  321.0 6.4 copy-start.7
  332.0 7.7 copy-start.2
  332.1 7.7 copy-start.8
  332.1 7.7 copy-start.30
  332.1 7.7 copy-start.32
  332.1 7.7 copy-start.33
  332.1 7.7 copy-start.41
  341.2 10.9 copy-start
  382.6 76.4 %all-to-all-start.2 = ((bf16[8,256,1536]{2,1,0:T(8,128)(2,1)}), bf16[8,256,1536]{2,1,0:T(8,128)(2,1)}, u32[]{:S(2)}, u32[]{:S(2)}) async-start(bf16[8,256,1536]{2,1,0:T(8,128)(2,1)} %get-tuple-element.568), calls=%async_computation.2 | async-start | bytes 12582912 | tf_op jit(solution)/shard_map/all_to_all | solution.py:305
  387.4 77.0 %all-gather.18.cloned.1.call-start = ((), (), s32[]{:S(2)}) async-start(), calls=%async_computation.19 | async-start | bytes 2949120 | tf_op jit(solution)/shard_map/all_gather | solution.py:120
  387.9 102.4 %all-gather.16.cloned.1.call-start = ((), (), s32[]{:S(2)}) async-start(), calls=%async_computation.18 | async-start | bytes 2949120 | tf_op jit(solution)/shard_map/all_gather | solution.py:119
  458.9 76.4 %all-to-all-start = ((bf16[8,256,1536]{2,1,0:T(8,128)(2,1)}), bf16[8,256,1536]{2,1,0:T(8,128)(2,1)}, u32[]{:S(2)}, u32[]{:S(2)}) async-start(bf16[8,256,1536]{2,1,0:T(8,128)(2,1)} %get-tuple-element.569), calls=%async_computation | async-start | bytes 12582912 | tf_op jit(solution)/shard_map/all_to_all | solution.py:243
  463.7 81.2 %all-gather.14.cloned.1.call-start = ((), (), s32[]{:S(2)}) async-start(), calls=%async_computation.17 | async-start | bytes 2949120 | tf_op jit(solution)/shard_map/all_gather | solution.py:118
  544.9 15.2 copy-start.46
  567.0 76.8 %all-to-all-start.1 = ((bf16[8,256,1536]{2,1,0:T(8,128)(2,1)}), bf16[8,256,1536]{2,1,0:T(8,128)(2,1)}, u32[]{:S(2)}, u32[]{:S(2)}) async-start(bf16[8,256,1536]{2,1,0:T(8,128)(2,1)} %convolution_convert_fusion), calls=%async_computation.1 | async-start | bytes 12582912 | tf_op jit(solution)/shard_map/all_to_all | solution.py:252
  572.3 8.2 copy-start.45
  572.3 8.2 copy-start.48
  587.9 61.0 %copy-start.17 = (bf16[256,1536]{1,0:T(8,128)(2,1)S(1)}, bf16[256,1536]{1,0:T(8,128)(2,1)}, u32[]{:S(2)}) copy-start(bf16[256,1536]{1,0:T(8,128)(2,1)} %param.35) | copy-start | bytes 2359300
  587.9 62.7 %copy-start.38 = (s32[1024]{0:T(1024)S(1)}, s32[1024]{0:T(1024)}, u32[]{:S(2)}) copy-start(s32[1024]{0:T(1024)} %copy-done.37) | copy-start | bytes 12292
  643.9 76.4 %all-to-all-start.3 = ((bf16[8,256,1536]{2,1,0:T(8,128)(2,1)}), bf16[8,256,1536]{2,1,0:T(8,128)(2,1)}, u32[]{:S(2)}, u32[]{:S(2)}) async-start(bf16[8,256,1536]{2,1,0:T(8,128)(2,1)} %add_convert_fusion), calls=%async_computation.3 | async-start | bytes 12582912 | tf_op jit(solution)/shard_map/all_to_all | solution.py:335
  648.7 215.5 %reduce-scatter.13.cloned.1.call-start = ((), (), s32[]{:S(2)}) async-start(), calls=%async_computation.20 | async-start | bytes 1179648 | tf_op jit(solution)/shard_map/reduce_scatter | solution.py:394
  738.0 15.0 slice-start
  745.7 7.2 slice-start.1
  756.7 4.0 copy-start.3
  756.7 4.0 copy-start.31
  763.0 3.7 copy-start.26
  770.4 4.7 copy-start.6
  786.6 4.7 copy-start.6
  802.9 4.7 copy-start.6
  819.2 4.7 copy-start.6
  829.5 74.4 %reduce-scatter.15.cloned.1.call-start = ((), (), s32[]{:S(2)}) async-start(), calls=%async_computation.21 | async-start | bytes 1179648 | tf_op jit(solution)/shard_map/reduce_scatter | solution.py:400
  832.9 121.1 %reduce-scatter.25.cloned.1.call-start = ((), (), s32[]{:S(2)}) async-start(), calls=%async_computation.26 | async-start | bytes 2949120 | tf_op jit(solution)/shard_map/reduce_scatter | solution.py:456
  842.3 161.6 %reduce-scatter.27.cloned.1.call-start = ((), (), s32[]{:S(2)}) async-start(), calls=%async_computation.27 | async-start | bytes 2949120 | tf_op jit(solution)/shard_map/reduce_scatter | solution.py:459
  852.1 9.6 copy-start.1
  852.1 201.7 %reduce-scatter.29.cloned.1.call-start = ((), (), s32[]{:S(2)}) async-start(), calls=%async_computation.28 | async-start | bytes 2949120 | tf_op jit(solution)/shard_map/reduce_scatter | solution.py:462
  861.6 3.7 copy-start.10
  861.6 3.7 copy-start.29
  861.6 3.7 copy-start.36
  861.6 292.3 %reduce-scatter.31.cloned.1.call-start = ((), (), s32[]{:S(2)}) async-start(), calls=%async_computation.29 | async-start | bytes 811008
  863.1 392.7 %reduce-scatter.19.cloned.1.call-start = ((), (), s32[]{:S(2)}) async-start(), calls=%async_computation.23 | async-start | bytes 1622016 | tf_op jit(solution)/shard_map/reduce_scatter | solution.py:449
  867.1 39.5 %copy-start.15 = (bf16[256,2,6,128]{0,3,2,1:T(8,128)(2,1)S(1)}, bf16[256,2,6,128]{0,3,2,1:T(8,128)(2,1)}, u32[]{:S(2)}) copy-start(bf16[256,2,6,128]{0,3,2,1:T(8,128)(2,1)} %convert_element_type.188) | copy-start | bytes 2359300
  867.1 490.6 %reduce-scatter.21.cloned.1.call-start = ((), (), s32[]{:S(2)}) async-start(), calls=%async_computation.24 | async-start | bytes 1622016 | tf_op jit(solution)/shard_map/reduce_scatter | solution.py:450
  906.5 592.2 %reduce-scatter.23.cloned.1.call-start = ((), (), s32[]{:S(2)}) async-start(), calls=%async_computation.25 | async-start | bytes 9732096 | tf_op jit(solution)/shard_map/reduce_scatter | solution.py:451
  913.1 727.8 %reduce-scatter.17.cloned.1.call-start = ((), (), s32[]{:S(2)}) async-start(), calls=%async_computation.22 | async-start | bytes 9732096 | tf_op jit(solution)/shard_map/reduce_scatter | solution.py:448
  1056.0 99.3 %copy-start.19 = (bf16[1536,256]{1,0:T(8,128)(2,1)S(1)}, bf16[1536,256]{1,0:T(8,128)(2,1)}, u32[]{:S(2)}) copy-start(bf16[1536,256]{1,0:T(8,128)(2,1)} %copy-done.18) | copy-start | bytes 2359300
  1061.1 96.1 %copy-start.21 = (bf16[1536,256]{1,0:T(8,128)(2,1)S(1)}, bf16[1536,256]{1,0:T(8,128)(2,1)}, u32[]{:S(2)}) copy-start(bf16[1536,256]{1,0:T(8,128)(2,1)} %copy-done.20) | copy-start | bytes 2359300
  1061.1 96.1 %copy-start.27 = (bf16[256,256]{1,0:T(8,128)(2,1)S(1)}, bf16[256,256]{1,0:T(8,128)(2,1)}, u32[]{:S(2)}) copy-start(bf16[256,256]{1,0:T(8,128)(2,1)} %reduce-scatter.15.cloned.1.call-done) | copy-start | bytes 393220
  1157.2 43.1 %copy-start.14 = (f32[256,1536]{1,0:T(8,128)S(1)}, f32[256,1536]{1,0:T(8,128)}, u32[]{:S(2)}) copy-start(f32[256,1536]{1,0:T(8,128)} %copy-done.13) | copy-start | bytes 4718596
  (31 other events, 87.8 us)
Sparse Core Ops, SparseCore 0:
  140.2 25.6 all-gather.7
  168.8 63.6 all-gather.9
  235.4 62.4 all-gather.11
  829.6 34.6 reduce-scatter.12
  867.8 35.9 reduce-scatter.14
  906.0 48.0 reduce-scatter.24
  956.4 47.5 reduce-scatter.26
  1006.3 47.5 reduce-scatter.28
  1058.9 94.9 reduce-scatter.30
  1159.6 96.0 reduce-scatter.18
  1261.6 96.0 reduce-scatter.20
  1364.0 134.6 reduce-scatter.22
  1506.2 134.6 reduce-scatter.16
Sparse Core Ops, SparseCore 1:
  389.4 50.8 all-gather.17
  441.7 48.6 all-gather.15
  491.8 48.6 all-gather.13
where the time goes:
time: 1660 us; the launch traced here: 1650 us
  waiting for transfers between devices  967 us (58%)
  matrix products  244 us (15%)
  blocking collectives  202 us (12%)
  local copies, waits for them, and re-layouts  116 us (7%)
  other arithmetic  81.1 us (5%)
  starting transfers between devices  20.6 us (1%)
  between operations  16.7 us (1%)
    reduce_scatter x1, waiting for transfers between devices, on_device(): lax.psum_scatter(query_w_grad, ('dp', 'expert'), scatter_dimension=0, til...  142 us
    reduce_scatter x1, waiting for transfers between devices, on_device(): lax.psum_scatter(out_grad, ('dp', 'expert'), scatter_dimension=0, tiled=T...  141 us
    reduce_scatter x1, waiting for transfers between devices, on_device(): lax.psum_scatter(value_w_grad, ('dp', 'expert'), scatter_dimension=0, til...  102 us
    unnamed x17, waiting for transfers between devices  96 us
    unnamed x2, blocking collectives  82.2 us
    all_to_all x1, waiting for transfers between devices, on_device(): lax.all_to_all(grad_outgoing, 'expert', split_axis=0, concat_axis=0, tile...  70.4 us
    all_to_all x1, waiting for transfers between devices, on_device(): lax.all_to_all(produced.reshape(group_size * local_experts, item_count, w...  55.9 us
    reduce_scatter x1, waiting for transfers between devices, on_device(): lax.psum_scatter(key_w_grad, ('dp', 'expert'), scatter_dimension=0, tiled...  52.7 us
  transfers between devices with their start and end apart: 20, of which 16 were waited for; matrix products, arithmetic and copies ran while one was open for 15% of the time, Pallas kernels for 0%

commit v1 on v0

v1 whole, which is shorter than its diff:
```python
import math

import jax
import jax.numpy as jnp
from jax import lax
from jax.sharding import PartitionSpec as P

QUERY_HEADS = 12
KEY_VALUE_HEADS = 2
HEAD_SIZE = 128


EPSILON = 1e-06
ROPE_BASE = 10000.0
MASKED_SCORE = -1e30
BF = jnp.bfloat16
F32 = jnp.float32


def rms_scale(values):
    return lax.rsqrt(jnp.mean(values * values, axis=-1, keepdims=True) + EPSILON)


def rope_tables(positions, half_size):
    angle_steps = lax.broadcasted_iota(F32, (half_size,), 0)
    frequency = jnp.exp(angle_steps * (-math.log(ROPE_BASE) / half_size))
    angles = positions.astype(F32)[:, None] * frequency
    return (jnp.cos(angles)[:, None, :], jnp.sin(angles)[:, None, :])


def apply_rotation(values, cosine_table, sine_table):
    half_size = values.shape[-1] // 2
    first = values[..., :half_size]
    second = values[..., half_size:]
    return jnp.concatenate(
        [first * cosine_table - second * sine_table, second * cosine_table + first * sine_table],
        axis=-1,
    )


def reverse_rotation(grads_in, cosine_table, sine_table):
    return apply_rotation(grads_in, cosine_table, -sine_table)


def seq_layout(lengths, seq_order):
    count_seq = lengths.shape[1]
    picked = seq_order[0][:, None] == lax.broadcasted_iota(jnp.int32, (count_seq, count_seq), 1)
    ordered = jnp.sum(jnp.where(picked, lengths[0][None, :], 0), axis=1)
    return (ordered, jnp.cumsum(ordered))


def seq_place(positions, ordered, seq_ends):
    passed = seq_ends[None, :] <= positions[:, None]
    sequence_index = jnp.sum(passed.astype(jnp.int32), axis=1)
    starts = jnp.sum(jnp.where(passed, ordered[None, :], 0), axis=1)
    return (sequence_index, positions - starts)


def block_scores(
    query_rows, key_portion, query_seq, query_stream, key_seq, key_stream, score_scale
):
    raw_scores = (
        jnp.einsum("tkrd,skd->krts", query_rows, key_portion, preferred_element_type=F32)
        * score_scale
    )
    allowed = (query_seq[:, None] == key_seq[None, :]) & (
        key_stream[None, :] <= query_stream[:, None]
    )
    return jnp.where(allowed, raw_scores, MASKED_SCORE)


def norm_backward(grad_normed, unit_values, inv_scale, gain_float):
    scaled = grad_normed * gain_float
    gain_grad = jnp.sum(grad_normed * unit_values, axis=0)
    input_grad = inv_scale * (
        scaled - unit_values * jnp.mean(scaled * unit_values, axis=-1, keepdims=True)
    )
    return (gain_grad, input_grad)


def dot(a, b):
    return jnp.dot(a, b, preferred_element_type=F32)


def dot_nt(a, b):
    return jnp.einsum("ac,bc->ab", a, b, preferred_element_type=F32)


def dot_tn(a, b):
    return jnp.einsum("ta,tb->ab", a, b, preferred_element_type=F32)


def on_device(
    tokens,
    lengths,
    seq_order,
    routes,
    norm_attn,
    w_query,
    key_projection,
    value_projection,
    w_out,
    norm_moe,
    w_router,
    w_gate,
    w_up,
    w_down,
    cotangent,
):
    token_count, width = tokens.shape
    n_experts = w_router.shape[1]
    rows = w_query.shape[0]
    group_size = lax.axis_size("expert")
    my_index = lax.axis_index("expert")
    query_per_key_heads = QUERY_HEADS // KEY_VALUE_HEADS
    kv_width = KEY_VALUE_HEADS * HEAD_SIZE
    q_width = QUERY_HEADS * HEAD_SIZE
    score_scale = 1.0 / math.sqrt(HEAD_SIZE)
    group_tokens = token_count * group_size

    small = jnp.concatenate(
        [
            w_router,
            norm_attn[:, None],
            norm_moe[:, None],
            jnp.zeros((rows, 128 - n_experts - 2), BF),
        ],
        axis=1,
    )
    pack = jnp.concatenate([w_query, key_projection, value_projection, small, w_out], axis=1)
    gate_w = lax.all_gather(w_gate[0], "dp", axis=0, tiled=True)
    up_w = lax.all_gather(w_up[0], "dp", axis=0, tiled=True)
    down_w = lax.all_gather(w_down[0], "dp", axis=0, tiled=True)
    pack = lax.all_gather(pack, ("dp", "expert"), axis=0, tiled=True)
    cot_all = lax.all_gather(cotangent, "expert", axis=0, tiled=True)
    c_k = q_width
    c_v = c_k + kv_width
    c_s = c_v + kv_width
    c_o = c_s + 128
    query_w = pack[:, :c_k]
    key_w = pack[:, c_k:c_v]
    value_w = pack[:, c_v:c_s]
    router_w = pack[:, c_s : c_s + n_experts]
    gain_one = pack[:, c_s + n_experts].astype(F32)
    gain_two = pack[:, c_s + n_experts + 1].astype(F32)
    out_w = pack[:, c_o:]

    seq_lens, seq_ends = seq_layout(lengths, seq_order)
    my_stream = lax.broadcasted_iota(jnp.int32, (token_count,), 0) * group_size + my_index
    query_seq, query_rel = seq_place(my_stream, seq_lens, seq_ends)
    all_rows = lax.broadcasted_iota(jnp.int32, (group_tokens,), 0)
    key_stream = all_rows % token_count * group_size + all_rows // token_count
    key_seq = seq_place(key_stream, seq_lens, seq_ends)[0]
    block_row_count = math.gcd(group_tokens, 512)
    block_count = group_tokens // block_row_count
    cosine_table, sine_table = rope_tables(query_rel, HEAD_SIZE // 2)
    inputs_float = tokens.astype(F32)
    inv_one = rms_scale(inputs_float)
    unit_one = inputs_float * inv_one
    normed_one = (unit_one * gain_one).astype(BF)
    query_pre = dot(normed_one, query_w)
    key_pre = dot(normed_one, key_w)
    value_pre = dot(normed_one, value_w)
    rotated_queries = (
        apply_rotation(
            query_pre.reshape(token_count, QUERY_HEADS, HEAD_SIZE), cosine_table, sine_table
        )
        .astype(BF)
        .reshape(token_count, KEY_VALUE_HEADS, query_per_key_heads, HEAD_SIZE)
    )
    rotated_keys = apply_rotation(
        key_pre.reshape(token_count, KEY_VALUE_HEADS, HEAD_SIZE),
        cosine_table,
        sine_table,
    ).astype(BF)
    key_value = jnp.concatenate(
        [rotated_keys.reshape(token_count, kv_width), value_pre.astype(BF)],
        axis=1,
    )
    gathered = lax.all_gather(key_value, "expert", axis=0, tiled=True)
    key_blocks = (
        gathered.reshape(block_count, block_row_count, 2 * kv_width),
        key_seq.reshape(block_count, block_row_count),
        key_stream.reshape(block_count, block_row_count),
    )

    def stats_step(carry, blocks):
        run_max, run_sum = carry
        key_value_block, seq_block, stream_block = blocks
        key_portion = key_value_block[:, :kv_width].reshape(-1, KEY_VALUE_HEADS, HEAD_SIZE)
        scores = block_scores(
            rotated_queries, key_portion, query_seq, my_stream, seq_block, stream_block, score_scale
        )
        new_max = jnp.maximum(run_max, jnp.max(scores, axis=-1))
        run_sum = run_sum * jnp.exp(run_max - new_max) + jnp.sum(
            jnp.exp(scores - new_max[..., None]), axis=-1
        )
        return ((new_max, run_sum), None)

    initial_maximum = jnp.full(
        (KEY_VALUE_HEADS, query_per_key_heads, token_count), MASKED_SCORE, F32
    )
    (row_max, row_sum), unused = lax.scan(
        stats_step, (initial_maximum, jnp.zeros_like(initial_maximum)), key_blocks
    )
    log_total = row_max + jnp.log(row_sum)

    def value_step(summed, blocks):
        key_value_block, seq_block, stream_block = blocks
        key_portion = key_value_block[:, :kv_width].reshape(-1, KEY_VALUE_HEADS, HEAD_SIZE)
        value_portion = key_value_block[:, kv_width:].reshape(-1, KEY_VALUE_HEADS, HEAD_SIZE)
        scores = block_scores(
            rotated_queries, key_portion, query_seq, my_stream, seq_block, stream_block, score_scale
        )
        low_chances = jnp.exp(scores - log_total[..., None]).astype(BF)
        summed = summed + jnp.einsum(
            "krts,skd->tkrd", low_chances, value_portion, preferred_element_type=F32
        )
        return (summed, None)

    empty_head_state = jnp.zeros(
        (token_count, KEY_VALUE_HEADS, query_per_key_heads, HEAD_SIZE), F32
    )
    attended, unused = lax.scan(value_step, empty_head_state, key_blocks)
    attended_low = attended.reshape(token_count, q_width).astype(BF)
    middle = inputs_float + dot(attended_low, out_w)
    inv_two = rms_scale(middle)
    unit_two = middle * inv_two
    normed_two = (unit_two * gain_two).astype(BF)

    logits = dot(normed_two, router_w)
    choose = jnp.any(
        routes[:, :, None] == lax.broadcasted_iota(jnp.int32, (1, 1, n_experts), 2), axis=1
    )
    top_logit = jnp.max(jnp.where(choose, logits, -jnp.inf), axis=1, keepdims=True)
    spread = jnp.where(choose, jnp.exp(jnp.minimum(logits - top_logit, 0.0)), 0.0)
    gates = spread / jnp.sum(spread, axis=1, keepdims=True)

    normed_all = lax.all_gather(normed_two, "expert", axis=0, tiled=True)
    gates_all = lax.all_to_all(
        gates.T.reshape(n_experts, 1, token_count), "expert", split_axis=0, concat_axis=1, tiled=True
    )
    gate_col = gates_all.reshape(group_tokens, 1)

    gate_pre = dot(normed_all, gate_w)
    up_pre = dot(normed_all, up_w)
    sig = jax.nn.sigmoid(gate_pre)
    silu = gate_pre * sig
    hidden = (silu * up_pre).astype(BF)
    returned = dot(hidden, down_w).astype(BF).astype(F32)
    cot_float = cot_all.astype(F32)
    grad_gates = jnp.sum(cot_float * returned, axis=1)
    weighted = (gate_col * returned).astype(BF)
    grad_returned = (gate_col * cot_float).astype(BF)
    grad_hidden = dot_nt(grad_returned, down_w)
    grad_gate_pre = (grad_hidden * up_pre * sig * (1.0 + gate_pre * (1.0 - sig))).astype(BF)
    grad_up_pre = (grad_hidden * silu).astype(BF)
    grad_row = (dot_nt(grad_gate_pre, gate_w) + dot_nt(grad_up_pre, up_w)).astype(BF)
    down_grad = dot_tn(hidden, grad_returned).astype(BF)
    gate_grad = dot_tn(normed_all, grad_gate_pre).astype(BF)
    up_grad = dot_tn(normed_all, grad_up_pre).astype(BF)

    grad_gates = lax.all_to_all(
        grad_gates.reshape(group_size, 1, token_count), "expert", split_axis=0, concat_axis=1, tiled=True
    ).reshape(n_experts, token_count).T
    row_sum_grad = lax.psum_scatter(grad_row, "expert", scatter_dimension=0, tiled=True)
    output = (
        middle + lax.psum_scatter(weighted, "expert", scatter_dimension=0, tiled=True).astype(F32)
    ).astype(BF)

    grad_out = cotangent.astype(F32)
    grad_logits = (
        gates * (grad_gates - jnp.sum(gates * grad_gates, axis=1, keepdims=True))
    ).astype(BF)
    router_grad = dot_tn(normed_two, grad_logits)
    grad_normed_two = dot_nt(grad_logits, router_w) + row_sum_grad.astype(F32)
    gain_two_grad, grad_middle = norm_backward(grad_normed_two, unit_two, inv_two, gain_two)
    grad_middle = grad_out + grad_middle
    grad_mixed = grad_middle.astype(BF)
    out_grad = dot_tn(attended_low, grad_mixed)
    grad_attended = dot_nt(grad_mixed, out_w).astype(BF)
    head_gradient = grad_attended.reshape(
        token_count, KEY_VALUE_HEADS, query_per_key_heads, HEAD_SIZE
    )
    row_dot = jnp.transpose(jnp.sum(head_gradient.astype(F32) * attended, axis=-1), (1, 2, 0))

    def grad_step(query_grad, blocks):
        key_value_block, seq_block, stream_block = blocks
        key_portion = key_value_block[:, :kv_width].reshape(-1, KEY_VALUE_HEADS, HEAD_SIZE)
        value_portion = key_value_block[:, kv_width:].reshape(-1, KEY_VALUE_HEADS, HEAD_SIZE)
        scores = block_scores(
            rotated_queries, key_portion, query_seq, my_stream, seq_block, stream_block, score_scale
        )
        chances = jnp.exp(scores - log_total[..., None])
        low_chances = chances.astype(BF)
        grad_chances = jnp.einsum(
            "tkrd,skd->krts", head_gradient, value_portion, preferred_element_type=F32
        )
        grad_scores = (chances * (grad_chances - row_dot[..., None])).astype(BF)
        query_grad = query_grad + jnp.einsum(
            "krts,skd->tkrd", grad_scores, key_portion, preferred_element_type=F32
        )
        key_terms = (
            jnp.einsum("krts,tkrd->skd", grad_scores, rotated_queries, preferred_element_type=F32)
            * score_scale
        )
        value_terms = jnp.einsum(
            "krts,tkrd->skd", low_chances, head_gradient, preferred_element_type=F32
        )
        return (query_grad, (key_terms.astype(BF), value_terms.astype(BF)))

    query_grad, (key_terms, value_terms) = lax.scan(grad_step, empty_head_state, key_blocks)
    query_grad = query_grad * score_scale
    kv_terms = jnp.concatenate(
        [key_terms.reshape(group_tokens, kv_width), value_terms.reshape(group_tokens, kv_width)],
        axis=1,
    )
    kv_mine = lax.psum_scatter(kv_terms, "expert", scatter_dimension=0, tiled=True)
    grad_query_pre = (
        reverse_rotation(
            query_grad.reshape(token_count, QUERY_HEADS, HEAD_SIZE), cosine_table, sine_table
        )
        .reshape(token_count, q_width)
        .astype(BF)
    )
    grad_key_pre = (
        reverse_rotation(
            kv_mine[:, :kv_width].astype(F32).reshape(token_count, KEY_VALUE_HEADS, HEAD_SIZE),
            cosine_table,
            sine_table,
        )
        .reshape(token_count, kv_width)
        .astype(BF)
    )
    grad_qkv = jnp.concatenate([grad_query_pre, grad_key_pre, kv_mine[:, kv_width:]], axis=1)
    grad_normed_one = dot_nt(grad_qkv, pack[:, :c_s])
    qkv_grad = dot_tn(normed_one, grad_qkv)
    gain_one_grad, grad_input = norm_backward(grad_normed_one, unit_one, inv_one, gain_one)
    tokens_grad = (grad_middle + grad_input).astype(BF)
    small_grad = jnp.concatenate(
        [
            router_grad,
            gain_one_grad[:, None],
            gain_two_grad[:, None],
            jnp.zeros((width, 128 - n_experts - 2), F32),
        ],
        axis=1,
    )
    pack_grad = jnp.concatenate(
        [qkv_grad.astype(BF), small_grad.astype(BF), out_grad.astype(BF)], axis=1
    )
    mine = lax.psum_scatter(pack_grad, ("dp", "expert"), scatter_dimension=0, tiled=True)
    mine = mine.astype(F32)
    gate_mine, up_mine, down_mine = (
        lax.psum_scatter(grad, "dp", scatter_dimension=0, tiled=True).astype(F32)[None]
        for grad in (gate_grad, up_grad, down_grad)
    )
    return (
        output,
        tokens_grad,
        mine[:, c_s + n_experts],
        mine[:, :c_k],
        mine[:, c_k:c_v],
        mine[:, c_v:c_s],
        mine[:, c_o:],
        mine[:, c_s + n_experts + 1],
        mine[:, c_s : c_s + n_experts],
        gate_mine,
        up_mine,
        down_mine,
    )


def solution(mesh):
    both = ("dp", "expert")
    return jax.shard_map(
        on_device,
        mesh=mesh,
        in_specs=(
            P(both, None),
            P("dp", None),
            P("dp", None),
            P(both, None),
            P(both),
            P(both, None),
            P(both, None),
            P(both, None),
            P(both, None),
            P(both),
            P(both, None),
            P("expert", "dp", None),
            P("expert", "dp", None),
            P("expert", "dp", None),
            P(both, None),
        ),
        out_specs=(
            P(both, None),
            P(both, None),
            P(both),
            P(both, None),
            P(both, None),
            P(both, None),
            P(both, None),
            P(both),
            P(both, None),
            P("expert", "dp", None),
            P("expert", "dp", None),
            P("expert", "dp", None),
        ),
        check_vma=False,
    )
```

time: 1660 us -> 1020 us (0.61)
  waiting for transfers between devices: 967 us -> 655 us
  blocking collectives: 202 us -> 0 us
  local copies, waits for them, and re-layouts: 116 us -> 65.5 us
  other arithmetic: 81.1 us -> 50.4 us
  matrix products: 244 us -> 216 us
    reduce_scatter x9 -> x7, waiting for transfers between devices: 606 us -> 372 us  [the longest x1 147 us: on_device(): lax.psum_scatter(pack_grad, ('dp', 'expert'), scatter_dimension=0, tiled=...]
    all_to_all x4 -> x2, waiting for transfers between devices: 214 us -> 4.56 us  [the longest x1 4.56 us: on_device(): lax.all_to_all(grad_gates.reshape(group_size, 1, token_count), 'expert',...]
    all_gather x5 -> x6, waiting for transfers between devices: 51.1 us -> 258 us  [the longest x1 90 us: on_device(): pack = lax.all_gather(pack, ('dp', 'expert'), axis=0, tiled=True)]
    all_gather x3 -> x0, blocking collectives: 120 us -> none  [the longest x1 42.7 us: on_device(): lax.all_gather(key_projection, ('dp', 'expert'), axis=0, tiled=True)]
    unnamed x17 -> x14, waiting for transfers between devices: 96 us -> 2.6 us
    unnamed x2 -> x0, blocking collectives: 82.2 us -> none
    gather x4 -> x0, local copies, waits for them, and re-layouts: 47.5 us -> none  [the longest x1 15.6 us: on_device(): grad_returned[source_row]]
    dot_general x27 -> x20, matrix products: 151 us -> 128 us  [the longest x6 47.6 us: dot_nt(): return jnp.einsum('ac,bc->ab', a, b, preferred_element_type=F32)]
  transfers between devices with their start and end apart: 20 -> 16, of which waited for: 16 -> 14; matrix products, arithmetic and copies ran while one was open for 15% -> 19% of each run, Pallas kernels for 0% -> 0%
where the time goes in v1:
time: 1020 us; the launch traced here: 1010 us
  waiting for transfers between devices  655 us (64%)
  matrix products  216 us (21%)
  local copies, waits for them, and re-layouts  65.5 us (6%)
  other arithmetic  50.4 us (5%)
  between operations  14.8 us (1%)
    reduce_scatter x1, waiting for transfers between devices, on_device(): lax.psum_scatter(pack_grad, ('dp', 'expert'), scatter_dimension=0, tiled=...  147 us
    reduce_scatter x3, waiting for transfers between devices, on_device(): lax.psum_scatter(grad, 'dp', scatter_dimension=0, tiled=True).astype(F32)  117 us
    all_gather x1, waiting for transfers between devices, on_device(): pack = lax.all_gather(pack, ('dp', 'expert'), axis=0, tiled=True)  90 us
    reduce_scatter x1, waiting for transfers between devices, on_device(): lax.psum_scatter(weighted, 'expert', scatter_dimension=0, tiled=True)  61.3 us
    dot_general x6, matrix products, dot_nt(): return jnp.einsum('ac,bc->ab', a, b, preferred_element_type=F32)  47.6 us
    all_gather x1, waiting for transfers between devices, on_device(): cot_all = lax.all_gather(cotangent, 'expert', axis=0, tiled=True)  46.2 us
    dot_general x8, matrix products, dot(): return jnp.dot(a, b, preferred_element_type=F32)  43.9 us
    all_gather x1, waiting for transfers between devices, on_device(): up_w = lax.all_gather(w_up[0], 'dp', axis=0, tiled=True)  42.4 us
  transfers between devices with their start and end apart: 16, of which 14 were waited for; matrix products, arithmetic and copies ran while one was open for 19% of the time, Pallas kernels for 0%

profile of v1, /device:TPU:0, one launch (start us, length us, event | category | flops | bytes accessed | tf_op | source)
XLA Modules:
  0.0 1011.5 jit_solution(10876324210970709593)
XLA Ops:
  15.0 90.0 %all-gather.11.cloned.1.call-done = bf16[1536,3712]{1,0:T(8,128)(2,1)} async-done(((bf16[48,3712]{1,0:T(8,128)(2,1)}), bf16[1536,3712]{1,0:T(8,128)(2,1)}) %all-gather.11.cloned.1.call-update) | async-done | bytes 11403280 | tf_op jit(solution)/shard_map/all_gather | solution.py:134
  105.0 2.3 convert_reduce_fusion
  114.4 4.4 fusion.55
  120.2 18.2 %all-gather.13.cloned.1.call-done = bf16[2048,512]{0,1:T(8,128)(2,1)} async-done(((bf16[256,512]{0,1:T(8,128)(2,1)}), bf16[2048,512]{0,1:T(8,128)(2,1)}) %all-gather.13.cloned.1.call-update) | async-done | bytes 2097168 | tf_op jit(solution)/shard_map/all_gather | solution.py:180
  140.2 36.4 %while.39 = (s32[]{:T(128)}, f32[2,6,256]{2,1,0:T(8,128)S(1)}, f32[2,6,256]{2,1,0:T(8,128)S(1)}, s32[256]{0:T(256)S(1)}, s32[4,512]{1,0:T(4,128)}, /*index=5*/s3...) while((s32[]{:T(128)}, f32[2,6,256]{2,1,0:T(8,128)S(1)}, ...), condition=%wide.region_9.10_spmd.clone, body=%wide.region_6.9_spmd.clone.sunk | while | flops 414072320 | bytes 15772812 | solution.py:203
  141.3 3.9 fusion.190
  145.1 4.4 exponential_reduce_fusion.2
  150.6 3.9 fusion.190
  154.5 4.1 exponential_reduce_fusion.2
  159.7 3.9 fusion.190
  163.5 4.1 exponential_reduce_fusion.2
  168.7 3.9 fusion.190
  172.5 4.1 exponential_reduce_fusion.2
  177.3 22.4 %while.40 = (s32[]{:T(128)}, f32[256,2,6,128]{0,3,2,1:T(8,128)}, bf16[4,512,512]{1,2,0:T(8,128)(2,1)S(1)}, s32[256]{0:T(256)S(1)}, s32[4,512]{1,0:T(4,128)}, /*i...) while((s32[]{:T(128)}, f32[256,2,6,128]{0,3,2,1:T(8,128)}, ...), condition=%wide.region_11.12_spmd.clone, body=%wide.region_10.11_spmd.clone.sunk | while | flops 812777984 | bytes 6843531 | solution.py:224
  178.3 4.0 bitcast_add_fusion.4
  183.4 4.7 bitcast_add_fusion.4
  189.1 4.7 bitcast_add_fusion.4
  194.9 4.7 bitcast_add_fusion.4
  201.9 4.3 multiply_reduce_fusion.3
  212.7 3.3 all-to-all-start
  216.3 37.9 %all-gather.15.cloned.1.call-done = bf16[2048,1536]{1,0:T(8,128)(2,1)} async-done(((bf16[256,1536]{1,0:T(8,128)(2,1)}), bf16[2048,1536]{1,0:T(8,128)(2,1)}) %all-gather.15.cloned.1.call-update) | async-done | bytes 6291472 | tf_op jit(solution)/shard_map/all_gather | solution.py:239
  254.2 9.5 fusion.81
  263.7 42.4 %all-gather.21.cloned.1.call-done = bf16[1,1536,768]{2,1,0:T(8,128)(2,1)} async-done(((bf16[1,384,768]{2,1,0:T(8,128)(2,1)}), bf16[1,1536,768]{2,1,0:T(8,128)(2,1)}) %all-gather.21.cloned.1.call-update) | async-done | bytes 2359312 | tf_op jit(solution)/shard_map/all_gather | solution.py:132
  306.1 9.5 fusion.77
  315.6 41.3 %all-gather.23.cloned.1.call-done = bf16[1,768,1536]{2,1,0:T(8,128)(2,1)} async-done(((bf16[1,192,1536]{2,1,0:T(8,128)(2,1)}), bf16[1,768,1536]{2,1,0:T(8,128)(2,1)}) %all-gather.23.cloned.1.call-update) | async-done | bytes 2359312 | tf_op jit(solution)/shard_map/all_gather | solution.py:133
  356.9 46.2 %all-gather.17.cloned.1.call-done = bf16[2048,1536]{1,0:T(8,128)(2,1)} async-done(((bf16[256,1536]{1,0:T(8,128)(2,1)}), bf16[2048,1536]{1,0:T(8,128)(2,1)}) %all-gather.17.cloned.1.call-update) | async-done | bytes 6291472 | tf_op jit(solution)/shard_map/all_gather | solution.py:135
  403.1 14.7 %multiply_convert_fusion = (bf16[2048,768]{1,0:T(8,128)(2,1)S(1)}, bf16[2048,768]{1,0:T(8,128)(2,1)S(1)}, bf16[2048,768]{1,0:T(8,128)(2,1)}) fusion(f32[2048,768]{1,0:T(8,128)} %fusion.81, f32[2048,768]{1,0:T(8,128)} %fusion.77, bf16[1,768,1536]{2,1,0:T(8,128)(2,1)} %all-gather.23.cloned.1.call-done, bf16[2048,1536]{1,0:T(8,128)(2,1)} %all-gather.17.cloned.1.call-done, ...), kind=kOutput, calls=%fused_computation.70 | convolution fusion | flops 4864868352 | bytes 30679040 | tf_op jit(solution)/shard_map/ac,bc->ab/dot_general | solution.py:86
  417.8 8.2 fusion.79
  426.0 9.8 add_convert_fusion
  437.5 11.0 %fusion.50 = (f32[2048]{0:T(1024)}, bf16[2048,1536]{1,0:T(8,128)(2,1)}) fusion(bf16[2048,1536]{1,0:T(8,128)(2,1)} %all-gather.17.cloned.1.call-done, f32[2048]{0:T(1024)S(1)} %bitcast.341, bf16[2048,768]{1,0:T(8,128)(2,1)} %get-tuple-element.637, bf16[1,768,1536]{2,1,0:T(8,128)(2,1)S(1)} %copy-done.38), kind=kOutput, calls=%fused_computation.62 | convolution fusion | flops 4853856256 | bytes 18104320 | tf_op jit(solution)/shard_map/dot_general | solution.py:82
  448.5 3.5 all-to-all-start.1
  452.1 4.6 all-to-all-done.1
  456.7 41.1 %reduce-scatter.10.cloned.1.call-done = bf16[256,1536]{1,0:T(8,128)(2,1)} async-done(((bf16[2048,1536]{1,0:T(8,128)(2,1)}), bf16[256,1536]{1,0:T(8,128)(2,1)}) %reduce-scatter.10.cloned.1.call-update) | async-done | bytes 786448 | tf_op jit(solution)/shard_map/reduce_scatter | solution.py:266
  497.8 4.2 multiply_reduce_fusion
  501.9 61.3 %reduce-scatter.8.cloned.1.call-done = bf16[256,1536]{1,0:T(8,128)(2,1)} async-done(((bf16[2048,1536]{1,0:T(8,128)(2,1)}), bf16[256,1536]{1,0:T(8,128)(2,1)}) %reduce-scatter.8.cloned.1.call-update) | async-done | bytes 786448 | tf_op jit(solution)/shard_map/reduce_scatter | solution.py:268
  563.3 3.5 multiply_add_fusion.3
  567.9 4.6 fusion.64
  577.3 69.1 %while.41 = (s32[]{:T(128)}, f32[256,2,6,128]{0,3,2,1:T(8,128)S(1)}, bf16[4,512,2,128]{3,1,2,0:T(8,128)(2,1)}, bf16[4,512,2,128]{3,1,2,0:T(8,128)(2,1)}, bf16[4,...) while((s32[]{:T(128)}, ...), condition=%wide.region_23.24_spmd.clone, body=%wide.region_22.23_spmd.clone.sunk | while | flops 2030567936 | bytes 92081504 | solution.py:312
  582.2 3.8 fusion.209
  586.0 2.8 bitcast_add_fusion.5
  588.9 3.6 fusion.210
  599.5 3.8 fusion.209
  603.3 2.8 bitcast_add_fusion.5
  606.2 3.6 fusion.210
  616.7 3.8 fusion.209
  620.6 2.8 bitcast_add_fusion.5
  623.4 3.6 fusion.210
  634.0 3.8 fusion.209
  637.9 2.8 bitcast_add_fusion.5
  640.7 3.6 fusion.210
  651.7 2.8 pad_maximum_fusion
  655.0 9.2 convolution_convert_fusion.5
  664.3 9.5 convolution_convert_fusion.4
  674.0 9.9 convolution_convert_fusion.3
  686.6 3.5 convolution_convert_fusion.2
  690.1 5.8 reduce-scatter.12.cloned.1.call-done
  697.0 6.1 fusion.89
  703.4 4.6 convolution_convert_fusion
  708.0 17.1 %concatenate.49 = bf16[1536,3712]{1,0:T(8,128)(2,1)} concatenate(bf16[1536,2048]{1,0:T(8,128)(2,1)} %convolution_convert_fusion, bf16[1536,8]{1,0:T(8,128)(2,1)S(1)} %copy.188, bf16[1536,1]{1,0:T(8,128)(2,1)S(1)} %broadcast_in_dim.174, bf16[1536,1]{1,0:T(8,128)(2,1)S(1)} %broadcast_in_dim.175, bf16[1536,118]{1,0:T(8,128)(2,1)S(1)} %broadcast_in_dim.156, ...), dimensions={1} | concatenate | bytes 22806528 | tf_op jit(solution)/shard_map/concatenate | solution.py:349
  725.1 21.3 %reduce-scatter.16.cloned.1.call-done = bf16[384,768]{1,0:T(8,128)(2,1)} async-done(((bf16[1536,768]{1,0:T(8,128)(2,1)}), bf16[384,768]{1,0:T(8,128)(2,1)}) %reduce-scatter.16.cloned.1.call-update) | async-done | bytes 589840 | tf_op jit(solution)/shard_map/reduce_scatter | solution.py:355
  748.5 47.7 %reduce-scatter.18.cloned.1.call-done = bf16[384,768]{1,0:T(8,128)(2,1)} async-done(((bf16[1536,768]{1,0:T(8,128)(2,1)}), bf16[384,768]{1,0:T(8,128)(2,1)}) %reduce-scatter.18.cloned.1.call-update) | async-done | bytes 589840 | tf_op jit(solution)/shard_map/reduce_scatter | solution.py:355
  798.4 47.8 %reduce-scatter.20.cloned.1.call-done = bf16[192,1536]{1,0:T(8,128)(2,1)} async-done(((bf16[768,1536]{1,0:T(8,128)(2,1)}), bf16[192,1536]{1,0:T(8,128)(2,1)}) %reduce-scatter.20.cloned.1.call-update) | async-done | bytes 589840 | tf_op jit(solution)/shard_map/reduce_scatter | solution.py:355
  848.4 2.7 fusion.88
  851.1 147.3 %reduce-scatter.14.cloned.1.call-done = bf16[48,3712]{1,0:T(8,128)(2,1)} async-done(((bf16[1536,3712]{1,0:T(8,128)(2,1)}), bf16[48,3712]{1,0:T(8,128)(2,1)}) %reduce-scatter.14.cloned.1.call-update) | async-done | bytes 356368 | tf_op jit(solution)/shard_map/reduce_scatter | solution.py:352
  (304 shorter events, 93.5 us)
Async XLA Ops:
  7.2 97.8 %all-gather.11.cloned.1.call-start = ((), (), s32[]{:S(2)}) async-start(), calls=%async_computation.9 | async-start | bytes 11759616 | tf_op jit(solution)/shard_map/all_gather | solution.py:134
  9.5 99.8 %copy-start.8 = (bf16[256,1536]{1,0:T(8,128)(2,1)S(1)}, bf16[256,1536]{1,0:T(8,128)(2,1)}, u32[]{:S(2)}) copy-start(bf16[256,1536]{1,0:T(8,128)(2,1)} %param.21) | copy-start | bytes 2359300
  11.5 127.0 %all-gather.13.cloned.1.call-start = ((), (), s32[]{:S(2)}) async-start(), calls=%async_computation.10 | async-start | bytes 2359296 | tf_op jit(solution)/shard_map/all_gather | solution.py:180
  14.0 100.3 %copy-start.28 = (f32[256]{0:T(256)}, f32[256]{0:T(256)S(1)}, u32[]{:S(2)}) copy-start(f32[256]{0:T(256)S(1)} %add_rsqrt_fusion.1) | copy-start | bytes 3076
  15.0 103.8 %copy-start.13 = (f32[256,64]{0,1:T(8,128)}, f32[256,64]{0,1:T(8,128)S(1)}, u32[]{:S(2)}) copy-start(f32[256,64]{0,1:T(8,128)S(1)} %get-tuple-element.658) | copy-start | bytes 196612
  107.3 7.1 copy-start.20
  111.7 104.6 %all-gather.19.cloned.1.call-start = ((), (), s32[]{:S(2)}) async-start(), calls=%async_computation.20 | async-start | bytes 2949120 | tf_op jit(solution)/shard_map/all_gather | solution.py:131
  112.5 141.7 %all-gather.15.cloned.1.call-start = ((), (), s32[]{:S(2)}) async-start(), calls=%async_computation.11 | async-start | bytes 7077888 | tf_op jit(solution)/shard_map/all_gather | solution.py:239
  199.6 6.6 copy-start.2
  201.9 4.4 copy-start.10
  201.9 5.5 copy-start.17
  206.3 4.2 copy-start.36
  208.5 97.6 %all-gather.21.cloned.1.call-start = ((), (), s32[]{:S(2)}) async-start(), calls=%async_computation.21 | async-start | bytes 2949120 | tf_op jit(solution)/shard_map/all_gather | solution.py:132
  209.1 147.7 %all-gather.23.cloned.1.call-start = ((), (), s32[]{:S(2)}) async-start(), calls=%async_computation.22 | async-start | bytes 2949120 | tf_op jit(solution)/shard_map/all_gather | solution.py:133
  209.7 193.4 %all-gather.17.cloned.1.call-start = ((), (), s32[]{:S(2)}) async-start(), calls=%async_computation.13 | async-start | bytes 7077888 | tf_op jit(solution)/shard_map/all_gather | solution.py:135
  212.0 285.7 %copy-start.22 = (f32[256]{0:T(256)}, f32[256]{0:T(256)S(1)}, u32[]{:S(2)}) copy-start(f32[256]{0:T(256)S(1)} %get-tuple-element.661) | copy-start | bytes 3076
  212.1 285.7 %copy-start.24 = (f32[256]{0:T(256)}, f32[256]{0:T(256)S(1)}, u32[]{:S(2)}) copy-start(f32[256]{0:T(256)S(1)} %fusion.117) | copy-start | bytes 3076
  212.7 190.4 %all-to-all-start = ((f32[8,1,256]{2,1,0:T(1,128)}), f32[8,1,256]{2,1,0:T(1,128)S(1)}, u32[]{:S(2)}, u32[]{:S(2)}) async-start(f32[8,1,256]{2,1,0:T(1,128)} %copy.178), calls=%async_computation | async-start | bytes 16384 | tf_op jit(solution)/shard_map/all_to_all | solution.py:240
  216.1 281.7 %reduce-scatter.10.cloned.1.call-start = ((), (), s32[]{:S(2)}) async-start(), calls=%async_computation.14 | async-start | bytes 7077888 | tf_op jit(solution)/shard_map/reduce_scatter | solution.py:266
  403.1 33.0 %copy-start.34 = (f32[8,1,256]{2,1,0:T(1,128)}, f32[8,1,256]{2,1,0:T(1,128)S(1)}, u32[]{:S(2)}) copy-start(f32[8,1,256]{2,1,0:T(1,128)S(1)} %all-to-all-done) | copy-start | bytes 24580
  403.1 14.7 %copy-start.37 = (bf16[1,1536,768]{2,1,0:T(8,128)(2,1)S(1)}, bf16[1,1536,768]{2,1,0:T(8,128)(2,1)}, u32[]{:S(2)}) copy-start(bf16[1,1536,768]{2,1,0:T(8,128)(2,1)} %all-gather.19.cloned.1.call-done) | copy-start | bytes 7077892
  417.8 8.2 copy-start.41
  417.8 8.2 copy-start.40
  417.8 8.2 copy-start.39
  435.9 127.4 %reduce-scatter.8.cloned.1.call-start = ((), (), s32[]{:S(2)}) async-start(), calls=%async_computation.12 | async-start | bytes 7077888 | tf_op jit(solution)/shard_map/reduce_scatter | solution.py:268
  448.5 114.8 %copy-start.12 = (bf16[256,1536]{1,0:T(8,128)(2,1)S(1)}, bf16[256,1536]{1,0:T(8,128)(2,1)}, u32[]{:S(2)}) copy-start(bf16[256,1536]{1,0:T(8,128)(2,1)} %param.35) | copy-start | bytes 2359300
  448.5 8.1 all-to-all-start.1
  452.0 243.9 %reduce-scatter.12.cloned.1.call-start = ((), (), s32[]{:S(2)}) async-start(), calls=%async_computation.15 | async-start | bytes 2359296 | tf_op jit(solution)/shard_map/reduce_scatter | solution.py:318
  456.7 110.1 %copy-start.18 = (f32[8,1,256]{2,1,0:T(1,128)}, f32[8,1,256]{2,1,0:T(1,128)S(1)}, u32[]{:S(2)}) copy-start(f32[8,1,256]{2,1,0:T(1,128)S(1)} %all-to-all-done.1) | copy-start | bytes 24580
  456.7 110.1 %copy-start.32 = (f32[256]{0:T(256)}, f32[256]{0:T(256)S(1)}, u32[]{:S(2)}) copy-start(f32[256]{0:T(256)S(1)} %fusion.112) | copy-start | bytes 3076
  578.4 3.7 copy-start.15
  578.5 3.7 copy-start.26
  578.5 3.7 copy-start.30
  586.0 6.4 copy-start.1
  588.9 3.6 copy-start.31
  595.7 3.7 copy-start.15
  595.7 3.7 copy-start.26
  595.7 3.7 copy-start.30
  603.3 6.4 copy-start.1
  606.2 3.6 copy-start.31
  613.0 3.7 copy-start.15
  613.0 3.7 copy-start.26
  613.0 3.7 copy-start.30
  620.6 6.4 copy-start.1
  623.4 3.6 copy-start.31
  630.3 3.7 copy-start.15
  630.3 3.7 copy-start.26
  630.3 3.7 copy-start.30
  637.9 6.4 copy-start.1
  640.7 3.6 copy-start.31
  654.5 91.8 %reduce-scatter.16.cloned.1.call-start = ((), (), s32[]{:S(2)}) async-start(), calls=%async_computation.17 | async-start | bytes 2949120 | tf_op jit(solution)/shard_map/reduce_scatter | solution.py:355
  664.3 9.7 copy-start.35
  664.3 131.9 %reduce-scatter.18.cloned.1.call-start = ((), (), s32[]{:S(2)}) async-start(), calls=%async_computation.18 | async-start | bytes 2949120 | tf_op jit(solution)/shard_map/reduce_scatter | solution.py:355
  673.9 10.3 %copy-start.7 = (bf16[256,1536]{1,0:T(8,128)(2,1)S(1)}, bf16[256,1536]{1,0:T(8,128)(2,1)}, u32[]{:S(2)}) copy-start(bf16[256,1536]{1,0:T(8,128)(2,1)} %multiply_convert_fusion.3) | copy-start | bytes 2359300
  673.9 10.3 %copy-start.19 = (f32[8,1,256]{2,1,0:T(1,128)S(1)}, f32[8,1,256]{2,1,0:T(1,128)}, u32[]{:S(2)}) copy-start(f32[8,1,256]{2,1,0:T(1,128)} %copy-done.18) | copy-start | bytes 24580
  673.9 10.3 %copy-start.23 = (f32[256]{0:T(256)S(1)}, f32[256]{0:T(256)}, u32[]{:S(2)}) copy-start(f32[256]{0:T(256)} %copy-done.22) | copy-start | bytes 3076
  673.9 10.3 %copy-start.25 = (f32[256]{0:T(256)S(1)}, f32[256]{0:T(256)}, u32[]{:S(2)}) copy-start(f32[256]{0:T(256)} %copy-done.24) | copy-start | bytes 3076
  673.9 10.3 %copy-start.33 = (f32[256]{0:T(256)S(1)}, f32[256]{0:T(256)}, u32[]{:S(2)}) copy-start(f32[256]{0:T(256)} %copy-done.32) | copy-start | bytes 3076
  673.9 172.3 %reduce-scatter.20.cloned.1.call-start = ((), (), s32[]{:S(2)}) async-start(), calls=%async_computation.19 | async-start | bytes 2949120 | tf_op jit(solution)/shard_map/reduce_scatter | solution.py:355
  684.0 314.5 %reduce-scatter.14.cloned.1.call-start = ((), (), s32[]{:S(2)}) async-start(), calls=%async_computation.16 | async-start | bytes 11759616 | tf_op jit(solution)/shard_map/reduce_scatter | solution.py:352
  686.6 10.4 %copy-start.9 = (bf16[256,1536]{1,0:T(8,128)(2,1)S(1)}, bf16[256,1536]{1,0:T(8,128)(2,1)}, u32[]{:S(2)}) copy-start(bf16[256,1536]{1,0:T(8,128)(2,1)} %param.21) | copy-start | bytes 2359300
  686.6 10.4 %copy-start.21 = (f32[1536]{0:T(1024)S(1)}, f32[1536]{0:T(1024)}, u32[]{:S(2)}) copy-start(f32[1536]{0:T(1024)} %copy-done.20) | copy-start | bytes 18436
  686.6 10.4 %copy-start.29 = (f32[256]{0:T(256)S(1)}, f32[256]{0:T(256)}, u32[]{:S(2)}) copy-start(f32[256]{0:T(256)} %copy-done.28) | copy-start | bytes 3076
  725.1 123.3 %copy-start.6 = (f32[256,1536]{1,0:T(8,128)S(1)}, f32[256,1536]{1,0:T(8,128)}, u32[]{:S(2)}) copy-start(f32[256,1536]{1,0:T(8,128)} %copy-done.4) | copy-start | bytes 4718596
  (12 other events, 20.8 us)
Sparse Core Ops, SparseCore 0:
  11.6 93.3 all-gather.10
  111.8 26.5 all-gather.12
  140.0 50.4 all-gather.18
  208.6 45.4 all-gather.14
  255.6 50.4 all-gather.20
  307.5 49.2 all-gather.22
  358.7 44.3 all-gather.16
  436.0 61.7 reduce-scatter.9
  501.5 61.7 reduce-scatter.7
  654.7 41.2 reduce-scatter.11
  698.3 48.0 reduce-scatter.15
  748.7 47.5 reduce-scatter.17
  798.6 47.5 reduce-scatter.19
  853.1 145.2 reduce-scatter.13

commit v2 on v1

--- a/solution.py
+++ b/solution.py
@@ -1,8 +1,11 @@
+import functools
 import math
 
 import jax
 import jax.numpy as jnp
 from jax import lax
+from jax.experimental import pallas as pl
+from jax.experimental.pallas import tpu as pltpu
 from jax.sharding import PartitionSpec as P
 
 QUERY_HEADS = 12
@@ -371,10 +374,903 @@
     )
 
 
+MESH_ID = pl.DeviceIdType.MESH
+ANY = pl.ANY
+LOG2E = math.log2(math.e)
+
+
+class Place:
+    def __init__(self):
+        d = lax.axis_index("dp")
+        e = lax.axis_index("expert")
+        core = lax.rem(e, 2)
+        x = lax.rem(lax.div(e, 2), 2)
+        y = lax.div(e, 4)
+        self.d, self.e, self.core = d, e, core
+        self.chip = lax.div(e, 2)
+        self.e_s = e + 1 - 2 * core
+        self.e_x = e + 2 - 4 * x
+        self.e_y = e + 4 - 8 * y
+        self.e_d = self.e_x + 4 - 8 * y
+        self.chip_x = self.chip + 1 - 2 * x
+        self.chip_y = self.chip + 2 - 4 * y
+        self.chip_d = self.chip_x + 2 - 4 * y
+        self.sib = (d, self.e_s)
+        self.nx = (d, self.e_x)
+        self.ny = (d, self.e_y)
+        half = lax.div(d, 2)
+        odd = lax.rem(d, 2)
+        self.pair = (2 * half + 1 - odd, e)
+        self.cross = (3 - d, e)
+        self.inner = (d == 1) | (d == 2)
+        self.order = (d, 2 * half + 1 - odd, 2 - half, 3 - 3 * half)
+
+    def greet(self):
+        barrier = pltpu.get_barrier_semaphore()
+        for other in (self.sib, self.nx, self.ny, self.pair):
+            pl.semaphore_signal(barrier, inc=1, device_id=other, device_id_type=MESH_ID)
+
+        @pl.when(self.inner)
+        def _():
+            pl.semaphore_signal(barrier, inc=1, device_id=self.cross, device_id_type=MESH_ID)
+            pl.semaphore_wait(barrier, 5)
+
+        @pl.when(jnp.logical_not(self.inner))
+        def _():
+            pl.semaphore_wait(barrier, 4)
+
+
+def rcopy(src, dst, send_sem, recv_sem, device):
+    return pltpu.make_async_remote_copy(
+        src_ref=src,
+        dst_ref=dst,
+        send_sem=send_sem,
+        recv_sem=recv_sem,
+        device_id=device,
+        device_id_type=MESH_ID,
+    )
+
+
+class PlaneGather:
+    def __init__(self, at, blk, half, send, recv):
+        self.at, self.blk, self.half, self.send, self.recv = at, blk, half, send, recv
+
+    def push(self, ref, target, slot_send, slot_recv, src=None):
+        rcopy(
+            ref if src is None else src, ref, self.send(slot_send), self.recv(slot_recv), target
+        ).start()
+
+    def await_(self, ref, slot):
+        rcopy(ref, ref, self.send(0), self.recv(slot), self.at.sib).wait_recv()
+
+    def sent(self, ref, slot):
+        rcopy(ref, ref, self.send(slot), self.recv(0), self.at.sib).wait_send()
+
+    def start(self, src=None):
+        at = self.at
+        own = self.blk(at.e)
+        self.push(own, at.nx, 0, 0, src)
+        self.push(own, at.ny, 1, 1, src)
+        self.push(own, at.sib, 2, 4, src)
+
+    def on_x(self):
+        at = self.at
+        got = self.blk(at.e_x)
+        self.await_(got, 0)
+        self.push(self.half(at.e_x, 0), at.ny, 3, 3)
+        self.push(got, at.sib, 4, 5)
+
+    def on_y(self):
+        at = self.at
+        got = self.blk(at.e_y)
+        self.await_(got, 1)
+        self.push(self.half(at.e_y, 1), at.nx, 5, 2)
+        self.push(got, at.sib, 6, 6)
+
+    def on_d(self):
+        at = self.at
+        self.await_(self.half(at.e_d, 1), 2)
+        self.await_(self.half(at.e_d, 0), 3)
+        self.push(self.blk(at.e_d), at.sib, 7, 7)
+
+    def on_s(self):
+        at = self.at
+        turn = at.e_s - at.e
+        self.await_(self.blk(at.e_s), 4)
+        self.await_(self.blk(at.e_x + turn), 5)
+        self.await_(self.blk(at.e_y + turn), 6)
+        self.await_(self.blk(at.e_d + turn), 7)
+
+    def drain(self):
+        at = self.at
+        whole = self.blk(at.e)
+        for slot in (0, 1, 2, 4, 6, 7):
+            self.sent(whole, slot)
+        self.sent(self.half(at.e, 0), 3)
+        self.sent(self.half(at.e, 1), 5)
+
+
+class LineGather:
+    def __init__(self, at, blk, send, recv):
+        self.at, self.blk, self.send, self.recv = at, blk, send, recv
+
+    def start(self, src=None):
+        at = self.at
+        own = self.blk(at.d)
+        from_ = own if src is None else src
+        rcopy(from_, own, self.send(0), self.recv(1), at.pair).start()
+
+        @pl.when(at.inner)
+        def _():
+            rcopy(from_, own, self.send(1), self.recv(2), at.cross).start()
+
+    def on(self, k):
+        at = self.at
+        got = self.blk(at.order[k])
+        rcopy(got, got, self.send(0), self.recv(k), at.pair).wait_recv()
+
+        @pl.when(at.inner)
+        def _():
+            if k == 1:
+                rcopy(got, got, self.send(2), self.recv(3), at.cross).start()
+            else:
+                rcopy(got, got, self.send(k + 1), self.recv(k), at.pair).start()
+
+    def drain(self):
+        at = self.at
+        own = self.blk(at.d)
+        rcopy(own, own, self.send(0), self.recv(0), at.pair).wait_send()
+
+        @pl.when(at.inner)
+        def _():
+            for slot in (1, 2, 3, 4):
+                rcopy(own, own, self.send(slot), self.recv(0), at.pair).wait_send()
+
+
+def rows_of(ref, start, size):
+    return ref.at[pl.ds(pl.multiple_of(start, 16), size)]
+
+
+def stream_facts(lens_ref, order_ref, token_count, group_size, e):
+    count = lens_ref.shape[1]
+    stream = lax.broadcasted_iota(jnp.int32, (token_count, 128), 0) * group_size + e
+    begin = jnp.zeros_like(stream)
+    end = jnp.int32(0)
+    for j in range(count):
+        size = jnp.int32(0)
+        for i in range(count):
+            size = size + jnp.where(order_ref[0, j] == i, lens_ref[0, i], 0)
+        end = end + size
+        begin = begin + jnp.where(stream >= end, size, 0)
+    return stream, begin, stream - begin
+
+
+def rotary(relative):
+    lane = lax.rem(lax.broadcasted_iota(jnp.int32, relative.shape, 1), HEAD_SIZE // 2)
+    frequency = jnp.exp(lane.astype(F32) * (-math.log(ROPE_BASE) / (HEAD_SIZE // 2)))
+    angles = relative.astype(F32) * frequency
+    first = lax.broadcasted_iota(jnp.int32, relative.shape, 1) < HEAD_SIZE // 2
+    sine = jnp.sin(angles)
+    return jnp.cos(angles), jnp.where(first, -sine, sine)
+
+
+def swap_halves(values):
+    return pltpu.roll(values, HEAD_SIZE // 2, 1)
+
+
+TILE = 64
+
+
+def tiles_of(i):
+    return range(max(0, i - 2), i + 1)
+
+
+def tile_bias(i, r, stream, begin, group_size):
+    wide = TILE * group_size
+    j = lax.broadcasted_iota(jnp.int32, (TILE, wide), 1)
+    key = (r * TILE + lax.rem(j, TILE)) * group_size + lax.div(j, TILE)
+    ok = key >= begin[i * TILE : (i + 1) * TILE, :1]
+    if r == i:
+        ok = ok & (key <= stream[i * TILE : (i + 1) * TILE, :1])
+    return jnp.where(ok, 0.0, MASKED_SCORE)
+
+
+def dot_nn(a, b):
+    return lax.dot_general(a, b, (((1,), (0,)), ((), ())), preferred_element_type=F32)
+
+
+def dot_bt(a, b):
+    return lax.dot_general(a, b, (((1,), (1,)), ((), ())), preferred_element_type=F32)
+
+
+def dot_at(a, b):
+    return lax.dot_general(a, b, (((0,), (0,)), ((), ())), preferred_element_type=F32)
+
+
+def column_as_row(small, lane):
+    pick = (lax.broadcasted_iota(jnp.int32, (8, 128), 1) == lane).astype(F32).astype(BF)
+    return dot_bt(pick, small)[:1]
+
+
+def front_kernel(
+    n_experts,
+    lens_ref,
+    order_ref,
+    tok_ref,
+    routes_ref,
+    pack_ref,
+    wo_ref,
+    gw_ref,
+    uw_ref,
+    dw_ref,
+    cot_ref,
+    x_all,
+    c_all,
+    gw_all,
+    uw_all,
+    dw_all,
+    pack_out,
+    wo_out,
+    kv_out,
+    q_out,
+    att_out,
+    lse_out,
+    mid_out,
+    pack_all,
+    wo_all,
+    kv_all,
+    unit_ref,
+    acc_ref,
+    pay_ref,
+    s_ref,
+    ag_send,
+    ag_recv,
+    z_send,
+    z_recv,
+    local,
+):
+    at = Place()
+    at.greet()
+    tokens, width = tok_ref.shape
+    shard = pack_ref.shape[0]
+    group = 8
+    kv_width = KEY_VALUE_HEADS * HEAD_SIZE
+    q_width = QUERY_HEADS * HEAD_SIZE
+    qkv = q_width + 2 * kv_width
+    per_kv = QUERY_HEADS // KEY_VALUE_HEADS
+    chunk = shard * group
+    cut_a = 9 * 128
+    cut_b = wo_ref.shape[1] // 2
+    items = {}
+
+    def add_item(name, blk, half):
+        n = len(items)
+        items[name] = PlaneGather(
+            at, blk, half, lambda k, n=n: ag_send.at[n, k], lambda k, n=n: ag_recv.at[n, k]
+        )
+
+    def add_weight(name, ref, z, cut):
+        wide = ref.shape[1]
+
+        def place(e):
+            return pl.ds(pl.multiple_of(z * chunk + e * shard, 16), shard)
+
+        def half(e, h):
+            return ref.at[place(e), pl.ds(0, cut) if h == 0 else pl.ds(cut, wide - cut)]
+
+        add_item(name, lambda e: ref.at[place(e)], half)
+
+    for k in range(4):
+        add_weight(("a", k), pack_all, at.order[k], cut_a)
+    for k in range(4):
+        add_weight(("b", k), wo_all, at.order[k], cut_b)
+    add_item("kv", lambda e: kv_all.at[e], lambda e, h: kv_all.at[e, :, pl.ds(h * kv_width, kv_width)])
+    part = tokens // 2
+    for name, ref, cut in (("x", x_all, 7 * 128), ("c", c_all, width // 2)):
+        wide = ref.shape[2]
+        for k in range(2):
+            rows = pl.ds(k * part, part)
+
+            def half(e, h, ref=ref, rows=rows, cut=cut, wide=wide):
+                return ref.at[e, rows, pl.ds(0, cut) if h == 0 else pl.ds(cut, wide - cut)]
+
+            add_item((name, k), lambda e, ref=ref, rows=rows: ref.at[e, rows], half)
+
+    lines = {}
+
+    def add_line(name, ref, size, start):
+        n = len(lines)
+        lines[name] = LineGather(
+            at,
+            lambda z: rows_of(ref, start(z), size),
+            lambda k, n=n: z_send.at[n, k],
+            lambda k, n=n: z_recv.at[n, k],
+        )
+
+    add_line("a", pack_all, shard, lambda z: z * chunk + at.e * shard)
+    add_line("b", wo_all, shard, lambda z: z * chunk + at.e * shard)
+    for name, ref, src in (("g", gw_all, gw_ref), ("u", uw_all, uw_ref), ("d", dw_all, dw_ref)):
+        size = src.shape[0]
+        add_line(name, ref, size, lambda z, size=size: z * size)
+
+    own_a = rows_of(pack_all, at.d * chunk + at.e * shard, shard)
+    own_b = rows_of(wo_all, at.d * chunk + at.e * shard, shard)
+    copies = [
+        pltpu.make_async_copy(pack_ref, own_a, local.at[0]),
+        pltpu.make_async_copy(wo_ref, own_b, local.at[1]),
+    ]
+    for n, (name, src) in enumerate((("g", gw_ref), ("u", uw_ref), ("d", dw_ref))):
+        copies.append(pltpu.make_async_copy(src, lines[name].blk(at.d), local.at[2 + n]))
+    for k in range(2):
+        rows = pl.ds(k * part, part)
+        copies.append(
+            pltpu.make_async_copy(cot_ref.at[rows], c_all.at[at.e, rows], local.at[5 + k])
+        )
+
+    lines["a"].start(pack_ref)
+    items["a", 0].start(pack_ref)
+    lines["b"].start(wo_ref)
+    for copy in copies:
+        copy.start()
+
+    tok = tok_ref[...].astype(F32)
+    scale_one = lax.rsqrt(jnp.mean(tok * tok, axis=1, keepdims=True) + EPSILON)
+    unit_ref[...] = tok * scale_one
+    stream, begin, relative = stream_facts(lens_ref, order_ref, tokens, group, at.e)
+    cosine, sine = rotary(relative)
+    acc_ref[...] = jnp.zeros_like(acc_ref)
+    copies[0].wait()
+    copies[1].wait()
+
+    def consume(k):
+        z = at.order[k]
+        place = pl.ds(pl.multiple_of(z * chunk, 128), chunk)
+        gain = column_as_row(pack_all[place, qkv:], n_experts)
+        normed = (unit_ref[:, place] * gain).astype(BF)
+        acc_ref[...] += dot_nn(normed, pack_all[place, :qkv])
+
+    lines["a"].on(1)
+    items["a", 1].start()
+    items["a", 0].on_x()
+    items["a", 0].on_y()
+    lines["g"].start(gw_ref)
+    items["a", 0].on_d()
+    lines["a"].on(2)
+    items["a", 2].start()
+    items["a", 1].on_x()
+    items["a", 1].on_y()
+    items["a", 0].on_s()
+    consume(0)
+    lines["a"].on(3)
+    items["a", 3].start()
+    lines["b"].on(1)
+    lines["u"].start(uw_ref)
+    lines["d"].start(dw_ref)
+    items["a", 1].on_d()
+    items["a", 2].on_x()
+    items["a", 2].on_y()
+    items["a", 1].on_s()
+    consume(1)
+    lines["b"].on(2)
+    items["a", 2].on_d()
+    items["a", 3].on_x()
+    items["a", 3].on_y()
+    items["b", 0].start()
+    items["a", 2].on_s()
+    consume(2)
+    lines["b"].on(3)
+    items["a", 3].on_d()
+    items["a", 3].on_s()
+    consume(3)
+    keep = [
+        pltpu.make_async_copy(pack_all, pack_out, local.at[7]),
+    ]
+    keep[0].start()
+
+    def turned(col):
+        v = acc_ref[:, col : col + HEAD_SIZE]
+        return (v * cosine + swap_halves(v) * sine).astype(BF)
+
+    for h in range(KEY_VALUE_HEADS):
+        kv_all[at.e, :, h * HEAD_SIZE : (h + 1) * HEAD_SIZE] = turned(q_width + h * HEAD_SIZE)
+    kv_all[at.e, :, kv_width:] = acc_ref[:, q_width + kv_width :].astype(BF)
+    items["kv"].start()
+    for h in range(QUERY_HEADS):
+        q_out[h] = turned(h * HEAD_SIZE)
+    items["b", 0].on_x()
+    items["b", 0].on_y()
+    items["b", 1].start()
+    items["kv"].on_x()
+    items["kv"].on_y()
+    items["b", 0].on_d()
+    items["b", 2].start()
+    items["kv"].on_d()
+    items["kv"].on_s()
+    keep.append(pltpu.make_async_copy(kv_all, kv_out, local.at[8]))
+    keep[1].start()
+
+    def step_b(n):
+        if n == 0:
+            items["b", 1].on_x()
+            items["b", 1].on_y()
+            items["b", 3].start()
+        elif n == 1:
+            items["b", 1].on_d()
+            items["b", 2].on_x()
+            items["b", 2].on_y()
+        elif n == 2:
+            items["b", 2].on_d()
+            items["b", 3].on_x()
+            items["b", 3].on_y()
+        elif n == 3:
+            items["b", 3].on_d()
+
+    factor = LOG2E / math.sqrt(HEAD_SIZE)
+    wide = TILE * group
+    for i in range(tokens // TILE):
+        step_b(i)
+        first = tiles_of(i)[0]
+        biases = [tile_bias(i, r, stream, begin, group) for r in tiles_of(i)]
+        here = slice(i * TILE, (i + 1) * TILE)
+        for g in range(KEY_VALUE_HEADS):
+            queries = q_out[g * per_kv : (g + 1) * per_kv, here, :].reshape(per_kv * TILE, HEAD_SIZE)
+            top = None
+            for r in tiles_of(i):
+                keys = kv_all[:, r * TILE : (r + 1) * TILE, g * HEAD_SIZE : (g + 1) * HEAD_SIZE]
+                s = dot_bt(queries, keys.reshape(wide, HEAD_SIZE)) * factor
+                s = s.reshape(per_kv, TILE, wide) + biases[r - first][None]
+                s = s.reshape(per_kv * TILE, wide)
+                s_ref[:, (r - first) * wide : (r - first + 1) * wide] = s
+                high = jnp.max(s, axis=1, keepdims=True)
+                top = high if top is None else jnp.maximum(top, high)
+            total = None
+            mixed = None
+            for r in tiles_of(i):
+                p = jnp.exp2(s_ref[:, (r - first) * wide : (r - first + 1) * wide] - top)
+                values = kv_all[
+                    :, r * TILE : (r + 1) * TILE, kv_width + g * HEAD_SIZE : kv_width + (g + 1) * HEAD_SIZE
+                ].reshape(wide, HEAD_SIZE)
+                row = jnp.sum(p, axis=1, keepdims=True)
+                term = dot_nn(p.astype(BF), values)
+                total = row if total is None else total + row
+                mixed = term if mixed is None else mixed + term
+            mixed = mixed / total
+            lse_out[g, i] = jnp.broadcast_to(top + jnp.log2(total), (per_kv * TILE, 128))
+            for h in range(per_kv):
+                col = (g * per_kv + h) * HEAD_SIZE
+                att_out[here, col : col + HEAD_SIZE] = mixed[h * TILE : (h + 1) * TILE]
+
+    for name in ("g", "u", "d"):
+        lines[name].on(1)
+    for k in range(4):
+        items["b", k].on_s()
+    keep.append(pltpu.make_async_copy(wo_all, wo_out, local.at[9]))
+    keep[2].start()
+    items["c", 0].start(cot_ref.at[pl.ds(0, part)])
+    attended = att_out[...].astype(BF)
+    step = 256
+    for n in range(width // step):
+        cols = slice(n * step, (n + 1) * step)
+        mid_out[:, cols] = tok_ref[:, cols].astype(F32) + dot_nn(attended, wo_all[:, cols])
+    middle = mid_out[...]
+    scale_two = lax.rsqrt(jnp.mean(middle * middle, axis=1, keepdims=True) + EPSILON)
+    small = pack_all[:, qkv:]
+    normed_two = (middle * scale_two * column_as_row(small, n_experts + 1)).astype(BF)
+    pay_ref[:, :width] = normed_two
+    logits = dot_nn(normed_two, small)
+    lane = lax.broadcasted_iota(jnp.int32, (tokens, 128), 1)
+    choose = lane == routes_ref[:, :1]
+    for k in range(1, routes_ref.shape[1]):
+        choose = choose | (lane == routes_ref[:, k : k + 1])
+    top = jnp.max(jnp.where(choose, logits, MASKED_SCORE), axis=1, keepdims=True)
+    spread = jnp.where(choose, jnp.exp(jnp.minimum(logits - top, 0.0)), 0.0)
+    gates = spread / jnp.sum(spread, axis=1, keepdims=True)
+    pay_ref[:, width:] = split_three(gates)
+    own_x = [
+        pltpu.make_async_copy(
+            pay_ref.at[pl.ds(k * part, part)], x_all.at[at.e, pl.ds(k * part, part)], local.at[10 + k]
+        )
+        for k in range(2)
+    ]
+    for k in range(2):
+        items["x", k].start(pay_ref.at[pl.ds(k * part, part)])
+        own_x[k].start()
+    for name in ("g", "u", "d"):
+        lines[name].on(2)
+    items["c", 0].on_x()
+    items["c", 0].on_y()
+    for k in range(2):
+        items["x", k].on_x()
+        items["x", k].on_y()
+    items["c", 1].start(cot_ref.at[pl.ds(part, part)])
+    items["c", 0].on_d()
+    for k in range(2):
+        items["x", k].on_d()
+    items["c", 1].on_x()
+    items["c", 1].on_y()
+    items["c", 1].on_d()
+    for name in ("g", "u", "d"):
+        lines[name].on(3)
+    for k in range(2):
+        items["c", k].on_s()
+        items["x", k].on_s()
+    for item in items.values():
+        item.drain()
+    for line in lines.values():
+        line.drain()
+    for copy in copies[2:] + keep + own_x:
+        copy.wait()
+
+
+def split_three(values):
+    high = values.astype(BF).astype(F32)
+    mid = (values - high).astype(BF).astype(F32)
+    low = values - high - mid
+    return (high + pltpu.roll(mid, 32, 1) + pltpu.roll(low, 64, 1)).astype(BF)
+
+
+def front(lengths, seq_order, tokens, routes, pack, wo, gw, uw, dw, cot, n_experts):
+    count, width = tokens.shape
+    group, line = 8, 4
+    kv_width = KEY_VALUE_HEADS * HEAD_SIZE
+    per_kv = QUERY_HEADS // KEY_VALUE_HEADS
+    sds = jax.ShapeDtypeStruct
+    smem = pl.BlockSpec(memory_space=pltpu.SMEM)
+    vmem = pl.BlockSpec(memory_space=pltpu.VMEM)
+    hbm = pl.BlockSpec(memory_space=ANY)
+    n_items = 13
+    return pl.pallas_call(
+        functools.partial(front_kernel, n_experts),
+        in_specs=[smem, smem] + [vmem] * 8,
+        out_specs=(hbm,) * 8 + (vmem,) * 4,
+        out_shape=(
+            sds((group, count, width + 128), BF),
+            sds((group, count, width), BF),
+            sds((line * gw.shape[0], gw.shape[1]), BF),
+            sds((line * uw.shape[0], uw.shape[1]), BF),
+            sds((line * dw.shape[0], dw.shape[1]), BF),
+            sds((width, pack.shape[1]), BF),
+            sds((width, wo.shape[1]), BF),
+            sds((group, count, 2 * kv_width), BF),
+            sds((QUERY_HEADS, count, HEAD_SIZE), BF),
+            sds((count, QUERY_HEADS * HEAD_SIZE), F32),
+            sds((KEY_VALUE_HEADS, count // TILE, per_kv * TILE, 128), F32),
+            sds((count, width), F32),
+        ),
+        scratch_shapes=[
+            pltpu.VMEM((width, pack.shape[1]), BF),
+            pltpu.VMEM((width, wo.shape[1]), BF),
+            pltpu.VMEM((group, count, 2 * kv_width), BF),
+            pltpu.VMEM((count, width), F32),
+            pltpu.VMEM((count, pack.shape[1] - 128), F32),
+            pltpu.VMEM((count, width + 128), BF),
+            pltpu.VMEM((per_kv * TILE, 3 * TILE * group), F32),
+            pltpu.SemaphoreType.DMA((n_items, 8)),
+            pltpu.SemaphoreType.DMA((n_items, 8)),
+            pltpu.SemaphoreType.DMA((5, 5)),
+            pltpu.SemaphoreType.DMA((5, 4)),
+            pltpu.SemaphoreType.DMA((12,)),
+        ],
+        compiler_params=pltpu.CompilerParams(
+            collective_id=1, has_side_effects=True, vmem_limit_bytes=60 * 2**20
+        ),
+    )(lengths, seq_order, tokens, routes, pack, wo, gw, uw, dw, cot)
+
+
+def moe_kernel(
+    x_ref, c_ref, gw, uw, dw, row_ref, out_ref, gg_ref, ug_ref, dg_ref, gacc, uacc, dacc, yacc, racc
+):
+    step = pl.program_id(0)
+    block = x_ref.shape[0]
+    width = c_ref.shape[1]
+    e = lax.axis_index("expert")
+    lane = lax.broadcasted_iota(jnp.int32, (block, 128), 1)
+    mine = (lane == e) | (lane == e + 32) | (lane == e + 64)
+    gate = jnp.sum(jnp.where(mine, x_ref[:, width:].astype(F32), 0.0), axis=1, keepdims=True)
+
+    @pl.when(step == 0)
+    def _():
+        gacc[...] = jnp.zeros_like(gacc)
+        uacc[...] = jnp.zeros_like(uacc)
+        dacc[...] = jnp.zeros_like(dacc)
+
+    grad_returned = (gate * c_ref[...].astype(F32)).astype(BF)
+    x = x_ref[:, :width]
+    part = 256
+    for f in range(gw.shape[1] // part):
+        cols = slice(f * part, (f + 1) * part)
+        gate_pre = dot_nn(x, gw[:, cols])
+        up_pre = dot_nn(x, uw[:, cols])
+        sig = 1.0 / (1.0 + jnp.exp(-gate_pre))
+        silu = gate_pre * sig
+        hidden = (silu * up_pre).astype(BF)
+        grad_hidden = dot_bt(grad_returned, dw[cols, :])
+        grad_up = (grad_hidden * silu).astype(BF)
+        grad_gate = (grad_hidden * up_pre * sig * (1.0 + gate_pre * (1.0 - sig))).astype(BF)
+        y = dot_nn(hidden, dw[cols, :])
+        r = dot_bt(grad_gate, gw[:, cols]) + dot_bt(grad_up, uw[:, cols])
+        if f == 0:
+            yacc[...] = y
+            racc[...] = r
+        else:
+            yacc[...] += y
+            racc[...] += r
+        dacc[cols, :] += dot_at(hidden, grad_returned)
+        gacc[:, cols] += dot_at(x, grad_gate)
+        uacc[:, cols] += dot_at(x, grad_up)
+    returned = yacc[...].astype(BF).astype(F32)
+    grad_gates = jnp.sum(c_ref[...].astype(F32) * returned, axis=1, keepdims=True)
+    out_ref[...] = (gate * returned).astype(BF)
+    row_ref[:, :width] = racc[...].astype(BF)
+    high = grad_gates.astype(BF).astype(F32)
+    row_ref[:, width:] = jnp.where(
+        lane == e, high, jnp.where(lane == e + 32, grad_gates - high, 0.0)
+    ).astype(BF)
+
+    @pl.when(step == pl.num_programs(0) - 1)
+    def _():
+        gg_ref[...] = gacc[...].astype(BF)
+        ug_ref[...] = uacc[...].astype(BF)
+        dg_ref[...] = dacc[...].astype(BF)
+
+
+def moe(x_all, c_all, gw, uw, dw):
+    rows, width = c_all.shape
+    hid = gw.shape[1]
+    block = 512
+
+    def full(*shape):
+        return pl.BlockSpec(shape, lambda i: (0, 0), pipeline_mode=pl.Buffered(1))
+
+    def moving(cols):
+        return pl.BlockSpec((block, cols), lambda i: (i, 0))
+
+    sds = jax.ShapeDtypeStruct
+    return pl.pallas_call(
+        moe_kernel,
+        grid=(rows // block,),
+        in_specs=[
+            moving(width + 128),
+            moving(width),
+            full(width, hid),
+            full(width, hid),
+            full(hid, width),
+        ],
+        out_specs=(
+            moving(width + 128),
+            moving(width),
+            full(width, hid),
+            full(width, hid),
+            full(hid, width),
+        ),
+        out_shape=(
+            sds((rows, width + 128), BF),
+            sds((rows, width), BF),
+            sds((width, hid), BF),
+            sds((width, hid), BF),
+            sds((hid, width), BF),
+        ),
+        scratch_shapes=[
+            pltpu.VMEM((width, hid), F32),
+            pltpu.VMEM((width, hid), F32),
+            pltpu.VMEM((hid, width), F32),
+            pltpu.VMEM((block, width), F32),
+            pltpu.VMEM((block, width), F32),
+        ],
+        compiler_params=pltpu.CompilerParams(vmem_limit_bytes=60 * 2**20),
+        cost_estimate=pl.CostEstimate(
+            flops=18 * rows * width * hid,
+            bytes_accessed=8 * rows * width + 12 * width * hid,
+            transcendentals=rows * hid,
+        ),
+    )(x_all, c_all, gw, uw, dw)
+
+
+def pack_weights(w_router, norm_attn, norm_moe, w_query, key_projection, value_projection):
+    rows, n_experts = w_router.shape
+    small = jnp.concatenate(
+        [
+            w_router,
+            norm_attn[:, None],
+            norm_moe[:, None],
+            jnp.zeros((rows, 128 - n_experts - 2), BF),
+        ],
+        axis=1,
+    )
+    return jnp.concatenate([w_query, key_projection, value_projection, small], axis=1)
+
+
+def on_device_fast(
+    tokens,
+    lengths,
+    seq_order,
+    routes,
+    norm_attn,
+    w_query,
+    key_projection,
+    value_projection,
+    w_out,
+    norm_moe,
+    w_router,
+    w_gate,
+    w_up,
+    w_down,
+    cotangent,
+):
+    token_count, width = tokens.shape
+    n_experts = w_router.shape[1]
+    group_size = lax.axis_size("expert")
+    my_index = lax.axis_index("expert")
+    per_kv = QUERY_HEADS // KEY_VALUE_HEADS
+    kv_width = KEY_VALUE_HEADS * HEAD_SIZE
+    q_width = QUERY_HEADS * HEAD_SIZE
+    score_scale = 1.0 / math.sqrt(HEAD_SIZE)
+    group_tokens = token_count * group_size
+    pack = pack_weights(w_router, norm_attn, norm_moe, w_query, key_projection, value_projection)
+    x_all, c_all, gw, uw, dw, pack, wo, kv_all, q_rot, attended, lse, middle = front(
+        lengths,
+        seq_order,
+        tokens,
+        routes,
+        pack,
+        w_out,
+        w_gate[0],
+        w_up[0],
+        w_down[0],
+        cotangent,
+        n_experts,
+    )
+    grad_row, weighted, gate_grad, up_grad, down_grad = moe(
+        x_all.reshape(group_tokens, width + 128), c_all.reshape(group_tokens, width), gw, uw, dw
+    )
+    c_k = q_width
+    c_v = c_k + kv_width
+    c_s = c_v + kv_width
+    router_w = pack[:, c_s : c_s + n_experts]
+    gain_one = pack[:, c_s + n_experts].astype(F32)
+    gain_two = pack[:, c_s + n_experts + 1].astype(F32)
+    seq_lens, seq_ends = seq_layout(lengths, seq_order)
+    my_stream = lax.broadcasted_iota(jnp.int32, (token_count,), 0) * group_size + my_index
+    query_seq, query_rel = seq_place(my_stream, seq_lens, seq_ends)
+    all_rows = lax.broadcasted_iota(jnp.int32, (group_tokens,), 0)
+    key_stream = all_rows % token_count * group_size + all_rows // token_count
+    key_seq = seq_place(key_stream, seq_lens, seq_ends)[0]
+    cosine_table, sine_table = rope_tables(query_rel, HEAD_SIZE // 2)
+    inputs_float = tokens.astype(F32)
+    inv_one = rms_scale(inputs_float)
+    unit_one = inputs_float * inv_one
+    normed_one = (unit_one * gain_one).astype(BF)
+    rotated_queries = q_rot.transpose(1, 0, 2).reshape(
+        token_count, KEY_VALUE_HEADS, per_kv, HEAD_SIZE
+    )
+    gathered = kv_all.reshape(group_tokens, 2 * kv_width)
+    log_total = (
+        lse[..., 0]
+        .reshape(KEY_VALUE_HEADS, token_count // TILE, per_kv, TILE)
+        .transpose(0, 2, 1, 3)
+        .reshape(KEY_VALUE_HEADS, per_kv, token_count)
+        / LOG2E
+    )
+    attended_low = attended.astype(BF)
+    attended = attended.reshape(token_count, KEY_VALUE_HEADS, per_kv, HEAD_SIZE)
+    inv_two = rms_scale(middle)
+    unit_two = middle * inv_two
+    own = lax.dynamic_slice_in_dim(x_all, my_index, 1, 0)[0]
+    normed_two = own[:, :width]
+    ext = own[:, width:].astype(F32)
+    gates = ext[:, :n_experts] + ext[:, 32 : 32 + n_experts] + ext[:, 64 : 64 + n_experts]
+
+    row_sum = lax.psum_scatter(grad_row, "expert", scatter_dimension=0, tiled=True)
+    row_sum_grad = row_sum[:, :width]
+    ext = row_sum[:, width:].astype(F32)
+    grad_gates = ext[:, :n_experts] + ext[:, 32 : 32 + n_experts]
+    output = (
+        middle + lax.psum_scatter(weighted, "expert", scatter_dimension=0, tiled=True).astype(F32)
+    ).astype(BF)
+
+    grad_out = cotangent.astype(F32)
+    grad_logits = (
+        gates * (grad_gates - jnp.sum(gates * grad_gates, axis=1, keepdims=True))
+    ).astype(BF)
+    router_grad = dot_tn(normed_two, grad_logits)
+    grad_normed_two = dot_nt(grad_logits, router_w) + row_sum_grad.astype(F32)
+    gain_two_grad, grad_middle = norm_backward(grad_normed_two, unit_two, inv_two, gain_two)
+    grad_middle = grad_out + grad_middle
+    grad_mixed = grad_middle.astype(BF)
+    out_grad = dot_tn(attended_low, grad_mixed)
+    head_gradient = (
+        dot_nt(grad_mixed, wo).astype(BF).reshape(token_count, KEY_VALUE_HEADS, per_kv, HEAD_SIZE)
+    )
+    row_dot = jnp.transpose(jnp.sum(head_gradient.astype(F32) * attended, axis=-1), (1, 2, 0))
+    key_portion = gathered[:, :kv_width].reshape(-1, KEY_VALUE_HEADS, HEAD_SIZE)
+    value_portion = gathered[:, kv_width:].reshape(-1, KEY_VALUE_HEADS, HEAD_SIZE)
+    scores = block_scores(
+        rotated_queries, key_portion, query_seq, my_stream, key_seq, key_stream, score_scale
+    )
+    chances = jnp.exp(scores - log_total[..., None])
+    grad_chances = jnp.einsum(
+        "tkrd,skd->krts", head_gradient, value_portion, preferred_element_type=F32
+    )
+    grad_scores = (chances * (grad_chances - row_dot[..., None])).astype(BF)
+    query_grad = (
+        jnp.einsum("krts,skd->tkrd", grad_scores, key_portion, preferred_element_type=F32)
+        * score_scale
+    )
+    key_terms = (
+        jnp.einsum("krts,tkrd->skd", grad_scores, rotated_queries, preferred_element_type=F32)
+        * score_scale
+    )
+    value_terms = jnp.einsum(
+        "krts,tkrd->skd", chances.astype(BF), head_gradient, preferred_element_type=F32
+    )
+    kv_terms = jnp.concatenate(
+        [
+            key_terms.reshape(group_tokens, kv_width).astype(BF),
+            value_terms.reshape(group_tokens, kv_width).astype(BF),
+        ],
+        axis=1,
+    )
+    kv_mine = lax.psum_scatter(kv_terms, "expert", scatter_dimension=0, tiled=True)
+    grad_query_pre = (
+        reverse_rotation(
+            query_grad.reshape(token_count, QUERY_HEADS, HEAD_SIZE), cosine_table, sine_table
+        )
+        .reshape(token_count, q_width)
+        .astype(BF)
+    )
+    grad_key_pre = (
+        reverse_rotation(
+            kv_mine[:, :kv_width].astype(F32).reshape(token_count, KEY_VALUE_HEADS, HEAD_SIZE),
+            cosine_table,
+            sine_table,
+        )
+        .reshape(token_count, kv_width)
+        .astype(BF)
+    )
+    grad_qkv = jnp.concatenate([grad_query_pre, grad_key_pre, kv_mine[:, kv_width:]], axis=1)
+    grad_normed_one = dot_nt(grad_qkv, pack[:, :c_s])
+    qkv_grad = dot_tn(normed_one, grad_qkv)
+    gain_one_grad, grad_input = norm_backward(grad_normed_one, unit_one, inv_one, gain_one)
+    tokens_grad = (grad_middle + grad_input).astype(BF)
+    small_grad = jnp.concatenate(
+        [
+            router_grad,
+            gain_one_grad[:, None],
+            gain_two_grad[:, None],
+            jnp.zeros((width, 128 - n_experts - 2), F32),
+        ],
+        axis=1,
+    )
+    pack_grad = jnp.concatenate(
+        [qkv_grad.astype(BF), small_grad.astype(BF), out_grad.astype(BF)], axis=1
+    )
+    mine = lax.psum_scatter(pack_grad, ("dp", "expert"), scatter_dimension=0, tiled=True)
+    mine = mine.astype(F32)
+    gate_mine, up_mine, down_mine = (
+        lax.psum_scatter(grad, "dp", scatter_dimension=0, tiled=True).astype(F32)[None]
+        for grad in (gate_grad, up_grad, down_grad)
+    )
+    return (
+        output,
+        tokens_grad,
+        mine[:, c_s + n_experts],
+        mine[:, :c_k],
+        mine[:, c_k:c_v],
+        mine[:, c_v:c_s],
+        mine[:, c_s + 128 :],
+        mine[:, c_s + n_experts + 1],
+        mine[:, c_s : c_s + n_experts],
+        gate_mine,
+        up_mine,
+        down_mine,
+    )
+
+
 def solution(mesh):
     both = ("dp", "expert")
+    small = mesh.shape["dp"] == 4 and mesh.shape["expert"] == 8
     return jax.shard_map(
-        on_device,
+        on_device_fast if small else on_device,
         mesh=mesh,
         in_specs=(
             P(both, None),

time: 1020 us -> 788 us (0.77)
  waiting for transfers between devices: 655 us -> 383 us
  Pallas kernels: 0 us -> 225 us
  matrix products: 216 us -> 83.5 us
  other arithmetic: 50.4 us -> 25.5 us
  local copies, waits for them, and re-layouts: 65.5 us -> 45.8 us
    all_gather x7 -> x0, waiting for transfers between devices: 276 us -> none  [the longest x1 90 us: on_device(): pack = lax.all_gather(pack, ('dp', 'expert'), axis=0, tiled=True)]
    pallas_call x0 -> x2, Pallas kernels: none -> 225 us  [the longest x1 169 us: front(): pl.pallas_call(functools.partial(front_kernel, n_experts), in_specs=[smem...]
    dot_general x28 -> x4, matrix products: 112 us -> 47 us  [the longest x1 18.3 us: on_device_fast(): jnp.einsum('tkrd,skd->krts', head_gradient, value_portion, preferred_elem...]
    dot_general x6 -> x3, matrix products: 47.6 us -> 14 us  [dot_nt(): return jnp.einsum('ac,bc->ab', a, b, preferred_element_type=F32)]
    dot_general x6 -> x3, matrix products: 37 us -> 9.62 us  [dot_tn(): return jnp.einsum('ta,tb->ab', a, b, preferred_element_type=F32)]
    reduce_sum x7 -> x3, other arithmetic: 18.9 us -> 1.75 us  [the longest x1 1.42 us: on_device_fast(): jnp.sum(head_gradient.astype(F32) * attended, axis=-1)]
  transfers between devices with their start and end apart: 16 -> 7, of which waited for: 14 -> 7; matrix products, arithmetic and copies ran while one was open for 19% -> 11% of each run, Pallas kernels for 0% -> 0%
where the time goes in v2:
time: 788 us; the launch traced here: 778 us
  waiting for transfers between devices  383 us (49%)
  Pallas kernels  225 us (29%)
  matrix products  83.5 us (11%)
  local copies, waits for them, and re-layouts  45.8 us (6%)
  other arithmetic  25.5 us (3%)
  between operations  14.8 us (2%)
    pallas_call x1, Pallas kernels, front(): pl.pallas_call(functools.partial(front_kernel, n_experts), in_specs=[smem...  169 us
    reduce_scatter x1, waiting for transfers between devices, on_device_fast(): lax.psum_scatter(pack_grad, ('dp', 'expert'), scatter_dimension=0, tiled=...  149 us
    reduce_scatter x3, waiting for transfers between devices, on_device_fast(): lax.psum_scatter(grad, 'dp', scatter_dimension=0, tiled=True).astype(F32)  114 us
    reduce_scatter x1, waiting for transfers between devices, on_device_fast(): lax.psum_scatter(weighted, 'expert', scatter_dimension=0, tiled=True)  61.4 us
    pallas_call x1, Pallas kernels, moe(): pl.pallas_call(moe_kernel, grid=(rows // block,), in_specs=[moving(width...  56.4 us
    reduce_scatter x1, waiting for transfers between devices, on_device_fast(): lax.psum_scatter(grad_row, 'expert', scatter_dimension=0, tiled=True)  32.5 us
    reduce_scatter x1, waiting for transfers between devices, on_device_fast(): lax.psum_scatter(kv_terms, 'expert', scatter_dimension=0, tiled=True)  24 us
    dot_general x1, matrix products, on_device_fast(): jnp.einsum('tkrd,skd->krts', head_gradient, value_portion, preferred_elem...  18.3 us
  transfers between devices with their start and end apart: 7, of which 7 were waited for; matrix products, arithmetic and copies ran while one was open for 11% of the time, Pallas kernels for 0%

profile of v2, /device:TPU:0, one launch (start us, length us, event | category | flops | bytes accessed | tf_op | source)
XLA Modules:
  0.0 777.9 jit_solution(16600894219464912570)
XLA Ops:
  7.2 0.8 copy.85
  8.0 0.8 copy.86
  8.8 0.8 copy.87
  9.5 1.5 copy.88.routes_ref
  11.0 1.7 concatenate.23.pack_ref
  12.7 169.0 %shard_map.238 = (bf16[8,256,1664]{2,1,0:T(8,128)(2,1)}, bf16[8,256,1536]{2,1,0:T(8,128)(2,1)}, bf16[1536,768]{1,0:T(8,128)(2,1)}, bf16[1536,768]{1,0:T(8,128)(2...) custom-call(s32[1,4]{1,0:T(1,128)} %lens_ref.1, ...), custom_call_target="tpu_custom_call" | custom-call | tf_op jit(solution)/shard_map/pallas_call | solution.py:922
  181.7 56.4 %shard_map.239 = (bf16[2048,1664]{1,0:T(8,128)(2,1)}, bf16[2048,1536]{1,0:T(8,128)(2,1)}, bf16[1536,768]{1,0:T(8,128)(2,1)}, bf16[1536,768]{1,0:T(8,128)(2,1)}, bf16[768,1536]{1,0:T(8,128)(2,1)}) custom-call(bf16[2048,1664]{1,0:T(8,128)(2,1)} %bitcast.123, bf16[2048,1536]{1,0:T(8,128)(2,1)} %bitcast.132, bf16[1536,768]{1,0:T(8,128)(2,1)} %get-tuple-element.32.gw, ...), custom_call_target="tpu_custom_call" | custom-call | flops 43486543872 | bytes 39321600 | tf_op jit(solution)/shard_map/pallas_call | solution.py:1029
  238.2 0.7 reduce-scatter.8.cloned.1.call-update
  239.0 0.7 copy-done.2
  239.6 1.6 copy.97
  241.2 2.6 fusion.54
  243.8 0.6 copy.124
  244.9 2.6 copy.125
  247.5 2.1 multiply_reduce_fusion.2
  250.0 1.8 convert_reduce_fusion
  252.0 1.3 dynamic-slice_bitcast_fusion
  253.4 0.9 copy-done.12
  254.3 2.3 compare_and_fusion
  256.6 12.9 %fusion.58 = f32[2,2048,256,6]{2,1,3,0:T(8,128)} fusion(bf16[2048,2,128,1]{0,2,3,1:T(8,128)(2,1)S(1)} %bitcast.101, bf16[256,2,6,128]{3,0,2,1:T(8,128)(2,1)S(1)} %bitcast.104), kind=kOutput, calls=%fused_computation.112 | convolution fusion | flops 1610612736 | bytes 27000832 | tf_op jit(solution)/shard_map/tkrd,skd->krts/dot_general | solution.py:66
  269.4 32.5 %reduce-scatter.10.cloned.1.call-done = bf16[256,1664]{1,0:T(8,128)(2,1)} async-done(((bf16[2048,1664]{1,0:T(8,128)(2,1)}), bf16[256,1664]{1,0:T(8,128)(2,1)}) %reduce-scatter.10.cloned.1.call-update) | async-done | bytes 851984 | tf_op jit(solution)/shard_map/reduce_scatter | solution.py:1163
  302.0 0.9 slice_convert_fusion
  302.9 0.2 multiply_reduce_fusion.5
  303.4 2.8 multiply_reduce_fusion
  306.2 61.4 %reduce-scatter.8.cloned.1.call-done = bf16[256,1536]{1,0:T(8,128)(2,1)} async-done(((bf16[2048,1536]{1,0:T(8,128)(2,1)}), bf16[256,1536]{1,0:T(8,128)(2,1)}) %reduce-scatter.8.cloned.1.call-update) | async-done | bytes 786448 | tf_op jit(solution)/shard_map/reduce_scatter | solution.py:1168
  367.5 3.2 multiply_add_fusion
  370.8 4.6 convolution_convert_fusion.2
  375.4 2.4 copy.94
  377.8 1.4 multiply_reduce_fusion.1
  379.3 12.5 %fusion.15 = bf16[2,128,2048]{2,1,0:T(8,128)(2,1)} fusion(bf16[256,2,6,128]{0,3,2,1:T(8,128)(2,1)S(1)} %bitcast.111, f32[2,2048,256,6]{2,1,3,0:T(8,128)} %fusion.58, f32[2,6,256]{2,1,0:T(8,128)S(1)} %reshape.277, pred[256,2048]{0,1:T(8,128)(4,1)S(1)} %copy-done.16), kind=kOutput, calls=%fused_computation.18 | convolution fusion | flops 1636302848 | bytes 27537408 | tf_op jit(solution)/shard_map/krts,tkrd->skd/dot_general | solution.py:1203
  391.8 18.3 %fusion.1 = bf16[2,6,256,2048]{2,3,1,0:T(8,128)(2,1)} fusion(f32[2,2048,256,6]{2,1,3,0:T(8,128)} %fusion.58, f32[2,6,256]{2,1,0:T(8,128)S(1)} %bitcast.124, f32[2,6,256]{2,1,0:T(8,128)S(1)} %reshape.277, pred[256,2048]{0,1:T(8,128)(4,1)} %compare_and_fusion, bf16[2048,2,128,1]{0,2,3,1:T(8,128)(2,1)} %bitcast.114, bf16[256,2,6,128]{0,3,2,1:T(8,128)(2,1)S(1)} %bitcast.112), kind=kOutput, calls=%fused_computation.2 | convolution fusion | flops 1648361472 | bytes 40132608 | tf_op jit(solution)/shard_map/tkrd,skd->krts/dot_general | solution.py:1191
  410.2 8.9 %fusion.14 = bf16[2,128,2048]{2,1,0:T(8,128)(2,1)S(1)} fusion(bf16[256,2,6,128]{3,0,2,1:T(8,128)(2,1)S(1)} %bitcast.105, bf16[2,6,256,2048]{2,3,1,0:T(8,128)(2,1)} %fusion.1), kind=kOutput, calls=%fused_computation.17 | convolution fusion | flops 1611661312 | bytes 14417920 | tf_op jit(solution)/shard_map/krts,tkrd->skd/dot_general | solution.py:1200
  419.1 1.6 pad_maximum_fusion
  420.7 0.5 reduce-scatter.18.cloned.1.call-update
  421.3 0.5 reduce-scatter.16.cloned.1.call-update
  421.9 0.5 reduce-scatter.20.cloned.1.call-update
  422.5 0.2 fusion.29
  422.7 0.3 multiply_cosine_fusion
  423.1 1.4 convolution_convert_fusion.3
  424.7 1.0 broadcast_in_dim.118
  425.8 7.3 convolution_multiply_fusion
  433.1 0.2 subtract_convert_fusion
  433.4 1.1 copy-done.3
  434.5 3.6 convolution_convert_fusion.1
  438.1 24.0 %reduce-scatter.12.cloned.1.call-done = bf16[256,512]{0,1:T(8,128)(2,1)} async-done(((bf16[2048,512]{0,1:T(8,128)(2,1)}), bf16[256,512]{0,1:T(8,128)(2,1)}) %reduce-scatter.12.cloned.1.call-update) | async-done | bytes 262160 | tf_op jit(solution)/shard_map/reduce_scatter | solution.py:1213
  462.0 1.0 fusion.57
  463.1 0.9 subtract_convert_fusion.1
  464.0 6.6 fusion.28
  470.6 1.0 broadcast_in_dim.117
  471.6 4.6 convolution_convert_fusion
  476.2 17.5 %concatenate.28 = bf16[1536,3712]{1,0:T(8,128)(2,1)} concatenate(bf16[1536,2048]{1,0:T(8,128)(2,1)} %convolution_convert_fusion, bf16[1536,8]{1,0:T(8,128)(2,1)S(1)} %copy.103, bf16[1536,1]{1,0:T(8,128)(2,1)} %broadcast_in_dim.117, bf16[1536,1]{1,0:T(8,128)(2,1)} %broadcast_in_dim.118, bf16[1536,118]{1,0:T(8,128)(2,1)S(1)} %broadcast_in_dim.107, ...), dimensions={1} | concatenate | bytes 22806528 | tf_op jit(solution)/shard_map/concatenate | solution.py:1244
  493.8 18.6 %reduce-scatter.18.cloned.1.call-done = bf16[384,768]{1,0:T(8,128)(2,1)} async-done(((bf16[1536,768]{1,0:T(8,128)(2,1)}), bf16[384,768]{1,0:T(8,128)(2,1)}) %reduce-scatter.18.cloned.1.call-update) | async-done | bytes 589840 | tf_op jit(solution)/shard_map/reduce_scatter | solution.py:1250
  512.4 2.2 bitcast_convert_fusion.1
  514.5 47.7 %reduce-scatter.16.cloned.1.call-done = bf16[384,768]{1,0:T(8,128)(2,1)} async-done(((bf16[1536,768]{1,0:T(8,128)(2,1)}), bf16[384,768]{1,0:T(8,128)(2,1)}) %reduce-scatter.16.cloned.1.call-update) | async-done | bytes 589840 | tf_op jit(solution)/shard_map/reduce_scatter | solution.py:1250
  562.2 2.2 bitcast_convert_fusion.2
  564.3 47.7 %reduce-scatter.20.cloned.1.call-done = bf16[192,1536]{1,0:T(8,128)(2,1)} async-done(((bf16[768,1536]{1,0:T(8,128)(2,1)}), bf16[192,1536]{1,0:T(8,128)(2,1)}) %reduce-scatter.20.cloned.1.call-update) | async-done | bytes 589840 | tf_op jit(solution)/shard_map/reduce_scatter | solution.py:1250
  612.0 2.3 bitcast_convert_fusion
  614.3 1.4 fusion.26
  615.7 148.7 %reduce-scatter.14.cloned.1.call-done = bf16[48,3712]{1,0:T(8,128)(2,1)} async-done(((bf16[1536,3712]{1,0:T(8,128)(2,1)}), bf16[48,3712]{1,0:T(8,128)(2,1)}) %reduce-scatter.14.cloned.1.call-update) | async-done | bytes 356368 | tf_op jit(solution)/shard_map/reduce_scatter | solution.py:1247
  764.4 1.0 convert_element_type.154
  765.4 0.7 slice_reduce_fusion
  766.1 0.7 slice.139
  766.8 0.7 copy.106
  767.5 1.8 fusion.55
  769.3 1.4 fusion.56
  (71 shorter events, 2.0 us)
Async XLA Ops:
  7.2 294.8 %reduce-scatter.10.cloned.1.call-start = ((), (), s32[]{:S(2)}) async-start(), calls=%async_computation.8 | async-start | bytes 7667712 | tf_op jit(solution)/shard_map/reduce_scatter | solution.py:1163
  238.1 129.4 %reduce-scatter.8.cloned.1.call-start = ((), (), s32[]{:S(2)}) async-start(), calls=%async_computation.7 | async-start | bytes 7077888 | tf_op jit(solution)/shard_map/reduce_scatter | solution.py:1168
  238.2 1.4 copy-start.2
  238.9 223.1 %reduce-scatter.12.cloned.1.call-start = ((), (), s32[]{:S(2)}) async-start(), calls=%async_computation.9 | async-start | bytes 2359296 | tf_op jit(solution)/shard_map/reduce_scatter | solution.py:1213
  243.8 0.7 copy-start.18
  243.8 0.7 copy-start.19
  244.5 12.1 %copy-start.4 = (bf16[2048,256]{0,1:T(8,128)(2,1)}, bf16[2048,256]{0,1:T(8,128)(2,1)S(1)}, u32[]{:S(2)}) copy-start(bf16[2048,256]{0,1:T(8,128)(2,1)S(1)} %copy.124) | copy-start | bytes 3145732
  244.9 7.0 copy-start.1
  251.8 4.7 copy-start.5
  253.3 0.9 copy-start.12
  302.0 1.4 copy-start.13
  375.4 2.4 copy-start.7
  377.8 1.4 copy-start.8
  377.8 1.5 copy-start.16
  379.3 12.5 %copy-start.9 = (bf16[256,1536]{0,1:T(8,128)(2,1)S(1)}, bf16[256,1536]{0,1:T(8,128)(2,1)}, u32[]{:S(2)}) copy-start(bf16[256,1536]{0,1:T(8,128)(2,1)} %copy.94) | copy-start | bytes 2359300
  391.8 18.3 %copy-start.6 = (bf16[12,256,128]{2,1,0:T(8,128)(2,1)S(1)}, bf16[12,256,128]{2,1,0:T(8,128)(2,1)}, u32[]{:S(2)}) copy-start(bf16[12,256,128]{2,1,0:T(8,128)(2,1)} %get-tuple-element.39) | copy-start | bytes 2359300
  410.2 8.9 %copy-start.11 = (bf16[2,128,2048]{2,1,0:T(8,128)(2,1)S(1)}, bf16[2,128,2048]{2,1,0:T(8,128)(2,1)}, u32[]{:S(2)}) copy-start(bf16[2,128,2048]{2,1,0:T(8,128)(2,1)} %fusion.15) | copy-start | bytes 3145732
  420.7 91.7 %reduce-scatter.18.cloned.1.call-start = ((), (), s32[]{:S(2)}) async-start(), calls=%async_computation.12 | async-start | bytes 2949120 | tf_op jit(solution)/shard_map/reduce_scatter | solution.py:1250
  421.2 140.9 %reduce-scatter.16.cloned.1.call-start = ((), (), s32[]{:S(2)}) async-start(), calls=%async_computation.11 | async-start | bytes 2949120 | tf_op jit(solution)/shard_map/reduce_scatter | solution.py:1250
  421.3 1.2 copy-start
  421.8 190.2 %reduce-scatter.20.cloned.1.call-start = ((), (), s32[]{:S(2)}) async-start(), calls=%async_computation.13 | async-start | bytes 2949120 | tf_op jit(solution)/shard_map/reduce_scatter | solution.py:1250
  422.4 342.0 %reduce-scatter.14.cloned.1.call-start = ((), (), s32[]{:S(2)}) async-start(), calls=%async_computation.10 | async-start | bytes 11759616 | tf_op jit(solution)/shard_map/reduce_scatter | solution.py:1247
  423.1 10.0 %copy-start.14 = (f32[256,64]{0,1:T(8,128)}, f32[256,64]{0,1:T(8,128)S(1)}, u32[]{:S(2)}) copy-start(f32[256,64]{0,1:T(8,128)S(1)} %get-tuple-element.118) | copy-start | bytes 196612
  423.1 10.0 %copy-start.15 = (f32[256,64]{0,1:T(8,128)}, f32[256,64]{0,1:T(8,128)S(1)}, u32[]{:S(2)}) copy-start(f32[256,64]{0,1:T(8,128)S(1)} %get-tuple-element.119) | copy-start | bytes 196612
  433.0 1.4 copy-start.3
  514.5 99.8 %copy-start.17 = (f32[256]{0:T(256)S(1)}, f32[256]{0:T(256)}, u32[]{:S(2)}) copy-start(f32[256]{0:T(256)} %get-tuple-element.99) | copy-start | bytes 3076
  612.0 2.3 copy-start.10
Sparse Core Ops, SparseCore 0:
  238.3 63.6 reduce-scatter.9
  305.7 61.7 reduce-scatter.7
  420.8 41.2 reduce-scatter.11
  464.3 48.0 reduce-scatter.17
  514.6 47.5 reduce-scatter.15
  564.4 47.5 reduce-scatter.19
  619.1 145.2 reduce-scatter.13

commit v3 on v2

--- a/solution.py
+++ b/solution.py
@@ -616,12 +616,12 @@
     att_out,
     lse_out,
     mid_out,
+    pay_ref,
     pack_all,
     wo_all,
     kv_all,
     unit_ref,
     acc_ref,
-    pay_ref,
     s_ref,
     ag_send,
     ag_recv,
@@ -922,7 +922,7 @@
     return pl.pallas_call(
         functools.partial(front_kernel, n_experts),
         in_specs=[smem, smem] + [vmem] * 8,
-        out_specs=(hbm,) * 8 + (vmem,) * 4,
+        out_specs=(hbm,) * 8 + (vmem,) * 5,
         out_shape=(
             sds((group, count, width + 128), BF),
             sds((group, count, width), BF),
@@ -936,6 +936,7 @@
             sds((count, QUERY_HEADS * HEAD_SIZE), F32),
             sds((KEY_VALUE_HEADS, count // TILE, per_kv * TILE, 128), F32),
             sds((count, width), F32),
+            sds((count, width + 128), BF),
         ),
         scratch_shapes=[
             pltpu.VMEM((width, pack.shape[1]), BF),
@@ -943,7 +944,6 @@
             pltpu.VMEM((group, count, 2 * kv_width), BF),
             pltpu.VMEM((count, width), F32),
             pltpu.VMEM((count, pack.shape[1] - 128), F32),
-            pltpu.VMEM((count, width + 128), BF),
             pltpu.VMEM((per_kv * TILE, 3 * TILE * group), F32),
             pltpu.SemaphoreType.DMA((n_items, 8)),
             pltpu.SemaphoreType.DMA((n_items, 8)),
@@ -1080,6 +1080,673 @@
     return jnp.concatenate([w_query, key_projection, value_projection, small], axis=1)
 
 
+class PlaneReduce:
+    def __init__(self, at, src, own, loader, seat, xs, ys, x2, y2, cut, send, recv):
+        self.at, self.src, self.own, self.loader = at, src, own, loader
+        self.seat, self.xs, self.ys, self.x2, self.y2 = seat, xs, ys, x2, y2
+        self.cut, self.send, self.recv = cut, send, recv
+
+    def copy(self, slot, src, dst, target):
+        return rcopy(src, dst, self.send(slot), self.recv(slot), target)
+
+    def moves(self):
+        at, own, cut = self.at, self.own, self.cut
+        low, high = pl.ds(0, cut), pl.ds(cut, self.seat.shape[-1] - cut)
+        return {
+            0: lambda: self.copy(0, self.src.at[:, 1 - at.core], self.seat, at.sib),
+            1: lambda: self.copy(1, own.at[at.chip_x, :, low], self.xs.at[0], at.nx),
+            2: lambda: self.copy(2, own.at[at.chip_d, :, low], self.xs.at[1], at.nx),
+            3: lambda: self.copy(3, own.at[at.chip_y, :, high], self.ys.at[0], at.ny),
+            4: lambda: self.copy(4, own.at[at.chip_d, :, high], self.ys.at[1], at.ny),
+            5: lambda: self.copy(5, own.at[at.chip_y, :, low], self.y2, at.ny),
+            6: lambda: self.copy(6, own.at[at.chip_x, :, high], self.x2, at.nx),
+        }
+
+    def begin(self, slot):
+        self.moves()[slot]().start()
+
+    def got(self, slot):
+        self.moves()[slot]().wait_recv()
+
+    def start(self):
+        self.begin(0)
+        if self.loader is not None:
+            self.loader.start()
+
+    def on_s(self):
+        if self.loader is not None:
+            self.loader.wait()
+        self.got(0)
+
+        def add(q, none):
+            self.own[q] = (self.own[q].astype(F32) + self.seat[q].astype(F32)).astype(BF)
+            return none
+
+        lax.fori_loop(0, 4, add, 0)
+        for slot in (1, 2, 3, 4):
+            self.begin(slot)
+
+    def on_xy(self):
+        at, own, cut = self.at, self.own, self.cut
+        self.got(1)
+        self.got(2)
+        own[at.chip_y, :, :cut] = (
+            own[at.chip_y, :, :cut].astype(F32) + self.xs[1].astype(F32)
+        ).astype(BF)
+        self.begin(5)
+        self.got(3)
+        self.got(4)
+        own[at.chip_x, :, cut:] = (
+            own[at.chip_x, :, cut:].astype(F32) + self.ys[1].astype(F32)
+        ).astype(BF)
+        self.begin(6)
+
+    def finish(self):
+        at, own, cut = self.at, self.own, self.cut
+        self.got(5)
+        low = own[at.chip, :, :cut].astype(F32) + self.xs[0].astype(F32) + self.y2[...].astype(F32)
+        self.got(6)
+        high = own[at.chip, :, cut:].astype(F32) + self.ys[0].astype(F32) + self.x2[...].astype(F32)
+        return low, high
+
+    def drain(self):
+        for slot in range(7):
+            self.moves()[slot]().wait_send()
+
+
+class LineReduce:
+    def __init__(self, at, blocks, near, far, send, recv):
+        self.at, self.blocks, self.near, self.far = at, blocks, near, far
+        self.send, self.recv = send, recv
+
+    def copy(self, slot, src, dst, target):
+        return rcopy(src, dst, self.send(slot), self.recv(slot), target)
+
+    def outer_moves(self):
+        at = self.at
+        return [
+            self.copy(n, self.blocks.at[at.order[n + 1]], self.near.at[n], at.pair)
+            for n in range(3)
+        ]
+
+    def cross_moves(self):
+        at = self.at
+        return [
+            self.copy(3 + n, self.blocks.at[at.order[n + 2]], self.far.at[n], at.cross)
+            for n in range(2)
+        ]
+
+    def back_move(self):
+        at = self.at
+        return self.copy(0, self.blocks.at[at.order[1]], self.near.at[0], at.pair)
+
+    def start(self):
+        at = self.at
+
+        @pl.when(jnp.logical_not(at.inner))
+        def _():
+            for move in self.outer_moves():
+                move.start()
+
+    def middle(self):
+        at, blocks = self.at, self.blocks
+
+        @pl.when(at.inner)
+        def _():
+            for n in range(2):
+                rcopy(
+                    self.near.at[n + 1], self.near.at[n + 1], self.send(0), self.recv(n + 1), at.pair
+                ).wait_recv()
+                blocks[at.order[n + 2]] = (
+                    blocks[at.order[n + 2]].astype(F32) + self.near[n + 1].astype(F32)
+                ).astype(BF)
+                self.cross_moves()[n].start()
+
+    def last(self):
+        at, blocks = self.at, self.blocks
+
+        @pl.when(at.inner)
+        def _():
+            self.cross_moves()[1].wait_recv()
+            blocks[at.order[1]] = (
+                blocks[at.order[1]].astype(F32) + self.far[1].astype(F32)
+            ).astype(BF)
+            self.back_move().start()
+
+    def finish(self, out):
+        at = self.at
+        self.back_move().wait_recv()
+        total = self.blocks[at.d].astype(F32) + self.near[0].astype(F32)
+
+        @pl.when(at.inner)
+        def _():
+            self.cross_moves()[0].wait_recv()
+            out[...] = total + self.far[0].astype(F32)
+            for move in self.cross_moves():
+                move.wait_send()
+            self.back_move().wait_send()
+
+        @pl.when(jnp.logical_not(at.inner))
+        def _():
+            out[...] = total
+            for move in self.outer_moves():
+                move.wait_send()
+
+
+def column_sums(values):
+    high = values.astype(BF)
+    low = (values - high.astype(F32)).astype(BF)
+    ones = jnp.ones((values.shape[0], 128), BF)
+    return dot_at(high, ones) + dot_at(low, ones)
+
+
+N_BACK = 18
+
+
+def back_kernel(
+    n_experts,
+    lens_ref,
+    order_ref,
+    row_in,
+    wgt_in,
+    tok_in,
+    q_in,
+    att_in,
+    lse_in,
+    mid_in,
+    cot_in,
+    kv_in,
+    pay_in,
+    pack_in,
+    wo_in,
+    output_ref,
+    tokens_grad_ref,
+    aq_out,
+    ak_out,
+    b_out,
+    own_ref,
+    seat_ref,
+    low1_ref,
+    high1_ref,
+    low2_ref,
+    high2_ref,
+    row_ref,
+    tok_ref,
+    q_ref,
+    att_ref,
+    lse_ref,
+    mid_ref,
+    cot_ref,
+    kv_ref,
+    pay_ref,
+    pack_ref,
+    wo_ref,
+    do_ref,
+    dkv_ref,
+    kseat,
+    klow1,
+    khigh1,
+    klow2,
+    khigh2,
+    bseat,
+    bhalf1,
+    bhalf2,
+    aseat,
+    ahalf1,
+    ahalf2,
+    cseat,
+    clow1,
+    chigh1,
+    clow2,
+    chigh2,
+    n1_ref,
+    dqkv_ref,
+    small_ref,
+    grad_middle_ref,
+    bz,
+    bnear,
+    bfar,
+    az,
+    anear,
+    afar,
+    cz,
+    cnear,
+    cfar,
+    r_send,
+    r_recv,
+    l_send,
+    l_recv,
+    local,
+    credit,
+):
+    at = Place()
+    at.greet()
+    tokens, width = tok_ref.shape
+    group = 8
+    kv_width = KEY_VALUE_HEADS * HEAD_SIZE
+    q_width = QUERY_HEADS * HEAD_SIZE
+    qkv = q_width + 2 * kv_width
+    per_kv = QUERY_HEADS // KEY_VALUE_HEADS
+    chunk = width // 4
+    shard = chunk // group
+    part = tokens // 2
+    red = {}
+
+    def sems(n):
+        return (lambda k: r_send.at[n, k]), (lambda k: r_recv.at[n, k])
+
+    cut_r = 7 * 128
+    for name, src, wide, cut in (("r", row_in, width + 128, cut_r), ("w", wgt_in, width, 6 * 128)):
+        for k in range(2):
+            send, recv = sems(len(red))
+            rows = pl.ds(k * part, part)
+            cols = pl.ds(0, wide)
+            mine = src.at[:, :, rows]
+            own = own_ref.at[k, :, :, cols]
+            red[name, k] = PlaneReduce(
+                at,
+                mine,
+                own,
+                pltpu.make_async_copy(mine.at[:, at.core], own, local.at[len(red)]),
+                seat_ref.at[k, :, :, cols],
+                low1_ref.at[k, :, :, pl.ds(0, cut)],
+                high1_ref.at[k, :, :, pl.ds(0, wide - cut)],
+                high2_ref.at[k, :, pl.ds(0, wide - cut)],
+                low2_ref.at[k, :, pl.ds(0, cut)],
+                cut,
+                send,
+                recv,
+            )
+    for k in range(2):
+        send, recv = sems(len(red))
+        rows = pl.ds(k * part, part)
+        mine = dkv_ref.at[:, :, rows]
+        red["k", k] = PlaneReduce(
+            at, mine, mine.at[:, at.core], None, kseat.at[k], klow1.at[k], khigh1.at[k],
+            khigh2.at[k], klow2.at[k], kv_width, send, recv,
+        )
+    for z in range(4):
+        send, recv = sems(len(red))
+        red["b", z] = PlaneReduce(
+            at, wo_ref.at[z], wo_ref.at[z, :, at.core], None, bseat.at[z], bhalf1.at[z, 0],
+            bhalf1.at[z, 1], bhalf2.at[z, 0], bhalf2.at[z, 1], width // 2, send, recv,
+        )
+    cols_q, cols_k = pl.ds(0, q_width), pl.ds(q_width, 2 * kv_width + 128)
+    for z in range(4):
+        send, recv = sems(len(red))
+        red["q", z] = PlaneReduce(
+            at, pack_ref.at[z, :, :, :, cols_q], pack_ref.at[z, :, at.core, :, cols_q], None,
+            aseat.at[z], ahalf1.at[z, 0], ahalf1.at[z, 1], ahalf2.at[z, 0], ahalf2.at[z, 1],
+            q_width // 2, send, recv,
+        )
+    for z in range(4):
+        send, recv = sems(len(red))
+        red["s", z] = PlaneReduce(
+            at, pack_ref.at[z, :, :, :, cols_k], pack_ref.at[z, :, at.core, :, cols_k], None,
+            cseat.at[z], clow1.at[z], chigh1.at[z], chigh2.at[z], clow2.at[z],
+            3 * 128, send, recv,
+        )
+    lines = {}
+    for n, (name, blocks, near, far) in enumerate(
+        (("b", bz, bnear, bfar), ("q", az, anear, afar), ("s", cz, cnear, cfar))
+    ):
+        lines[name] = LineReduce(
+            at, blocks, near, far, lambda k, n=n: l_send.at[n, k], lambda k, n=n: l_recv.at[n, k]
+        )
+
+    red["r", 0].start()
+    red["r", 1].start()
+    loads = {}
+    for n, (name, src, dst) in enumerate(
+        (
+            ("pay", pay_in, pay_ref),
+            ("mid", mid_in, mid_ref),
+            ("cot", cot_in, cot_ref),
+            ("pack", pack_in, pack_ref),
+            ("wo", wo_in, wo_ref),
+            ("att", att_in, att_ref),
+            ("lse", lse_in, lse_ref),
+            ("q", q_in, q_ref),
+            ("kv", kv_in, kv_ref),
+            ("tok", tok_in, tok_ref),
+        )
+    ):
+        loads[name] = pltpu.make_async_copy(src, dst, local.at[4 + n])
+        loads[name].start()
+    stream, begin, relative = stream_facts(lens_ref, order_ref, tokens, group, at.e)
+    cosine, sine = rotary(relative)
+    red["r", 0].on_s()
+    red["r", 1].on_s()
+    for name in ("tok", "pack"):
+        loads[name].wait()
+
+    def tok_unit():
+        tok = tok_ref[...].astype(F32)
+        scale = lax.rsqrt(jnp.mean(tok * tok, axis=1, keepdims=True) + EPSILON)
+        return tok * scale, scale
+
+    small = pack_ref[..., qkv:].reshape(width, 128)
+    gain_one = column_as_row(small, n_experts)
+    gain_two = column_as_row(small, n_experts + 1)
+    n1_ref[...] = (tok_unit()[0] * gain_one).astype(BF)
+    for k in range(2):
+        red["r", k].on_xy()
+    for name in ("pay", "mid", "cot"):
+        loads[name].wait()
+    for k in range(2):
+        rows = slice(k * part, (k + 1) * part)
+        low, high = red["r", k].finish()
+        row_ref[rows, :cut_r] = low
+        row_ref[rows, cut_r:] = high
+    for k in range(2):
+        red["r", k].drain()
+    for other in (at.sib, at.nx, at.ny):
+        pl.semaphore_signal(credit, inc=1, device_id=other, device_id_type=MESH_ID)
+
+    lane = lax.broadcasted_iota(jnp.int32, (tokens, 128), 1)
+    ext = pay_ref[:, width:].astype(F32)
+    gates = jnp.where(
+        lane < n_experts, ext + pltpu.roll(ext, 96, 1) + pltpu.roll(ext, 64, 1), 0.0
+    )
+    ext = row_ref[:, width:]
+    grad_gates = jnp.where(lane < n_experts, ext + pltpu.roll(ext, 96, 1), 0.0)
+    weighted_sum = jnp.sum(gates * grad_gates, axis=1, keepdims=True)
+    grad_logits = (gates * (grad_gates - weighted_sum)).astype(BF)
+    grad_normed = dot_bt(grad_logits, small) + row_ref[:, :width]
+    middle = mid_ref[...]
+    scale_two = lax.rsqrt(jnp.mean(middle * middle, axis=1, keepdims=True) + EPSILON)
+    unit_two = middle * scale_two
+    inner_sum = jnp.mean(grad_normed * gain_two * unit_two, axis=1, keepdims=True)
+    grad_middle = cot_ref[...].astype(F32) + scale_two * (
+        grad_normed * gain_two - unit_two * inner_sum
+    )
+    products = grad_normed * unit_two
+    pl.semaphore_wait(credit, 3)
+    red["w", 0].start()
+    loads["wo"].wait()
+    grad_middle_ref[...] = grad_middle
+    mixed = grad_middle.astype(BF)
+    for z in range(4):
+        heads = dot_bt(mixed, wo_ref[z].reshape(chunk, width)).astype(BF)
+        for j in range(chunk // HEAD_SIZE):
+            do_ref[z * (chunk // HEAD_SIZE) + j] = heads[:, j * HEAD_SIZE : (j + 1) * HEAD_SIZE]
+    loads["att"].wait()
+    for z in range(4):
+        left = att_ref[:, z * chunk : (z + 1) * chunk].astype(BF)
+        wo_ref[z] = dot_at(left, mixed).astype(BF).reshape(4, 2, shard, width)
+        red["b", z].start()
+    lane_small = lax.broadcasted_iota(jnp.int32, (width, 128), 1)
+    small_ref[...] = dot_at(pay_ref[:, :width], grad_logits) + jnp.where(
+        lane_small == n_experts + 1, column_sums(products), 0.0
+    )
+    for name in ("lse", "q", "kv"):
+        loads[name].wait()
+    row_ref[:, :width] = jnp.zeros((tokens, width), F32)
+    n_tiles = tokens // TILE
+    wide = TILE * group
+    for g in range(KEY_VALUE_HEADS):
+        for i in range(n_tiles):
+            here = slice(i * TILE, (i + 1) * TILE)
+            dots = []
+            for h in range(per_kv):
+                col = (g * per_kv + h) * HEAD_SIZE
+                dots.append(
+                    jnp.sum(
+                        do_ref[g * per_kv + h, here, :].astype(F32)
+                        * att_ref[here, col : col + HEAD_SIZE],
+                        axis=1,
+                        keepdims=True,
+                    )
+                )
+            dots = jnp.concatenate(dots, axis=0)
+            lse_ref[g, i, :, 64:] = jnp.broadcast_to(dots, (per_kv * TILE, 64))
+    red["w", 0].on_s()
+    for z in range(4):
+        red["b", z].on_s()
+
+    factor = LOG2E / math.sqrt(HEAD_SIZE)
+    score_scale = 1.0 / math.sqrt(HEAD_SIZE)
+
+    def attend_back(r):
+        queries_of = [i for i in range(n_tiles) if r in tiles_of(i)]
+        biases = {i: tile_bias(i, r, stream, begin, group) for i in queries_of}
+        there = slice(r * TILE, (r + 1) * TILE)
+        for g in range(KEY_VALUE_HEADS):
+            key_cols = slice(g * HEAD_SIZE, (g + 1) * HEAD_SIZE)
+            value_cols = slice(kv_width + g * HEAD_SIZE, kv_width + (g + 1) * HEAD_SIZE)
+            heads = slice(g * per_kv, (g + 1) * per_kv)
+            keys = kv_ref[:, there, key_cols].reshape(wide, HEAD_SIZE)
+            values = kv_ref[:, there, value_cols].reshape(wide, HEAD_SIZE)
+            grad_keys = None
+            grad_values = None
+            for i in queries_of:
+                here = slice(i * TILE, (i + 1) * TILE)
+                queries = q_ref[heads, here, :].reshape(per_kv * TILE, HEAD_SIZE)
+                grads = do_ref[heads, here, :].reshape(per_kv * TILE, HEAD_SIZE)
+                s = dot_bt(queries, keys) * factor
+                s = (s.reshape(per_kv, TILE, wide) + biases[i][None]).reshape(per_kv * TILE, wide)
+                p = jnp.exp2(s - lse_ref[g, i, :, :1])
+                ds = (p * (dot_bt(grads, values) - lse_ref[g, i, :, 64:65])).astype(BF)
+                term_k = dot_at(ds, queries)
+                term_v = dot_at(p.astype(BF), grads)
+                grad_keys = term_k if grad_keys is None else grad_keys + term_k
+                grad_values = term_v if grad_values is None else grad_values + term_v
+                grad_queries = dot_nn(ds, keys)
+                for h in range(per_kv):
+                    col = (g * per_kv + h) * HEAD_SIZE
+                    row_ref[here, col : col + HEAD_SIZE] += grad_queries[
+                        h * TILE : (h + 1) * TILE
+                    ]
+            dkv_ref[:, :, there, key_cols] = (
+                (grad_keys * score_scale).astype(BF).reshape(4, 2, TILE, HEAD_SIZE)
+            )
+            dkv_ref[:, :, there, value_cols] = grad_values.astype(BF).reshape(4, 2, TILE, HEAD_SIZE)
+
+    def settle(name, z, blocks, cut):
+        low, high = red[name, z].finish()
+        blocks[z, :, :cut] = low.astype(BF)
+        blocks[z, :, cut:] = high.astype(BF)
+
+    attend_back(0)
+    for z in range(4):
+        red["b", z].on_xy()
+    attend_back(1)
+    red["k", 0].start()
+    red["w", 0].on_xy()
+    attend_back(2)
+    red["k", 0].on_s()
+    for z in range(4):
+        settle("b", z, bz, width // 2)
+    lines["b"].start()
+    attend_back(3)
+    red["k", 1].start()
+    red["k", 0].on_xy()
+
+    def output_part(k):
+        rows = slice(k * part, (k + 1) * part)
+        low, high = red["w", k].finish()
+        output_ref[rows, : 6 * 128] = (mid_ref[rows, : 6 * 128] + low).astype(BF)
+        output_ref[rows, 6 * 128 :] = (mid_ref[rows, 6 * 128 :] + high).astype(BF)
+
+    def turned_back(v):
+        return (v * cosine - swap_halves(v) * sine).astype(BF)
+
+    for h in range(QUERY_HEADS):
+        cols = slice(h * HEAD_SIZE, (h + 1) * HEAD_SIZE)
+        dqkv_ref[:, cols] = turned_back(row_ref[:, cols] * score_scale)
+    red["k", 1].on_s()
+    grad_q = dqkv_ref[:, :q_width]
+    for z in range(4):
+        cols = slice(z * chunk, (z + 1) * chunk)
+        att_ref[:, cols] = dot_bt(grad_q, pack_ref[z, :, :, :, :q_width].reshape(chunk, q_width))
+        pack_ref[z, :, :, :, :q_width] = (
+            dot_at(n1_ref[:, cols], grad_q).astype(BF).reshape(4, 2, shard, q_width)
+        )
+        red["q", z].start()
+        if z == 0:
+            red["k", 1].on_xy()
+    for k in range(2):
+        rows = slice(k * part, (k + 1) * part)
+        low, high = red["k", k].finish()
+        row_ref[rows, :kv_width] = low
+        row_ref[rows, kv_width : 2 * kv_width] = high
+    lines["b"].middle()
+    for z in range(4):
+        red["q", z].on_s()
+    for h in range(KEY_VALUE_HEADS):
+        v = row_ref[:, h * HEAD_SIZE : (h + 1) * HEAD_SIZE]
+        dqkv_ref[:, q_width + h * HEAD_SIZE : q_width + (h + 1) * HEAD_SIZE] = turned_back(v)
+    dqkv_ref[:, q_width + kv_width :] = row_ref[:, kv_width : 2 * kv_width].astype(BF)
+    grad_kv = dqkv_ref[:, q_width:]
+    for z in range(4):
+        cols = slice(z * chunk, (z + 1) * chunk)
+        att_ref[:, cols] += dot_bt(
+            grad_kv, pack_ref[z, :, :, :, q_width:qkv].reshape(chunk, 2 * kv_width)
+        )
+        pack_ref[z, :, :, :, q_width:qkv] = (
+            dot_at(n1_ref[:, cols], grad_kv).astype(BF).reshape(4, 2, shard, 2 * kv_width)
+        )
+    unit_one, scale_one = tok_unit()
+    grad_one = att_ref[...]
+    small_ref[...] += jnp.where(lane_small == n_experts, column_sums(grad_one * unit_one), 0.0)
+    pack_ref[..., qkv:] = small_ref[...].astype(BF).reshape(4, 4, 2, shard, 128)
+    for z in range(4):
+        red["s", z].start()
+    lines["b"].last()
+    for z in range(4):
+        red["q", z].on_xy()
+    for z in range(4):
+        red["s", z].on_s()
+    inner_sum = jnp.mean(grad_one * gain_one * unit_one, axis=1, keepdims=True)
+    back_one = scale_one * (grad_one * gain_one - unit_one * inner_sum)
+    tokens_grad_ref[...] = (grad_middle_ref[...] + back_one).astype(BF)
+    red["w", 1].start()
+    for z in range(4):
+        settle("q", z, az, q_width // 2)
+    lines["q"].start()
+    for z in range(4):
+        red["s", z].on_xy()
+    red["w", 1].on_s()
+    for z in range(4):
+        settle("s", z, cz, 3 * 128)
+    lines["s"].start()
+    lines["q"].middle()
+    lines["s"].middle()
+    output_part(0)
+    red["w", 1].on_xy()
+    lines["q"].last()
+    lines["s"].last()
+    lines["b"].finish(b_out)
+    output_part(1)
+    lines["q"].finish(aq_out)
+    lines["s"].finish(ak_out)
+    for key, item in red.items():
+        if key[0] != "r":
+            item.drain()
+
+
+def back(
+    lengths, seq_order, row, weighted, tokens, q_rot, att, lse, middle, cot, kv, pay, pack, wo, n_experts
+):
+    count, width = tokens.shape
+    group = 8
+    shard = width // 32
+    kv_width = KEY_VALUE_HEADS * HEAD_SIZE
+    part = count // 2
+    wide_r, cut_r = width + 128, 7 * 128
+    wide_s, cut_s = 2 * kv_width + 128, 3 * 128
+    half = width // 2
+    sds = jax.ShapeDtypeStruct
+    smem = pl.BlockSpec(memory_space=pltpu.SMEM)
+    vmem = pl.BlockSpec(memory_space=pltpu.VMEM)
+    hbm = pl.BlockSpec(memory_space=ANY)
+    row = row.reshape(4, 2, count, wide_r)
+    weighted = weighted.reshape(4, 2, count, width)
+    pack = pack.reshape(4, 4, 2, shard, pack.shape[1])
+    wo = wo.reshape(4, 4, 2, shard, width)
+
+    def low(*shape):
+        return pltpu.VMEM(shape, BF)
+
+    def like(a):
+        return pltpu.VMEM(a.shape, a.dtype)
+
+    return pl.pallas_call(
+        functools.partial(back_kernel, n_experts),
+        in_specs=[smem, smem] + [hbm] * 12,
+        out_specs=(vmem,) * 5,
+        out_shape=(
+            sds((count, width), BF),
+            sds((count, width), BF),
+            sds((shard, width), F32),
+            sds((shard, wide_s), F32),
+            sds((shard, width), F32),
+        ),
+        scratch_shapes=[
+            low(2, 4, part, wide_r),
+            low(2, 4, part, wide_r),
+            low(2, 2, part, cut_r),
+            low(2, 2, part, wide_r - cut_r),
+            low(2, part, cut_r),
+            low(2, part, wide_r - cut_r),
+            pltpu.VMEM((count, wide_r), F32),
+            like(tokens),
+            like(q_rot),
+            like(att),
+            like(lse),
+            like(middle),
+            like(cot),
+            like(kv),
+            like(pay),
+            like(pack),
+            like(wo),
+            like(q_rot),
+            low(4, 2, count, 2 * kv_width),
+            low(2, 4, part, 2 * kv_width),
+            low(2, 2, part, kv_width),
+            low(2, 2, part, kv_width),
+            low(2, part, kv_width),
+            low(2, part, kv_width),
+            low(4, 4, shard, width),
+            low(4, 2, 2, shard, half),
+            low(4, 2, shard, half),
+            low(4, 4, shard, width),
+            low(4, 2, 2, shard, half),
+            low(4, 2, shard, half),
+            low(4, 4, shard, wide_s),
+            low(4, 2, shard, cut_s),
+            low(4, 2, shard, wide_s - cut_s),
+            low(4, shard, cut_s),
+            low(4, shard, wide_s - cut_s),
+            low(count, width),
+            low(count, width + 2 * kv_width),
+            pltpu.VMEM((width, 128), F32),
+            pltpu.VMEM((count, width), F32),
+            low(4, shard, width),
+            low(3, shard, width),
+            low(2, shard, width),
+            low(4, shard, width),
+            low(3, shard, width),
+            low(2, shard, width),
+            low(4, shard, wide_s),
+            low(3, shard, wide_s),
+            low(2, shard, wide_s),
+            pltpu.SemaphoreType.DMA((N_BACK, 7)),
+            pltpu.SemaphoreType.DMA((N_BACK, 7)),
+            pltpu.SemaphoreType.DMA((3, 5)),
+            pltpu.SemaphoreType.DMA((3, 5)),
+            pltpu.SemaphoreType.DMA((14,)),
+            pltpu.SemaphoreType.REGULAR,
+        ],
+        compiler_params=pltpu.CompilerParams(
+            collective_id=2, has_side_effects=True, vmem_limit_bytes=63 * 2**20
+        ),
+        cost_estimate=pl.CostEstimate(
+            flops=15 * 10**10, bytes_accessed=5 * 10**7, transcendentals=10**7
+        ),
+    )(lengths, seq_order, row, weighted, tokens, q_rot, att, lse, middle, cot, kv, pay, pack, wo)
+
+
 def on_device_fast(
     tokens,
     lengths,
@@ -1099,15 +1766,10 @@
 ):
     token_count, width = tokens.shape
     n_experts = w_router.shape[1]
-    group_size = lax.axis_size("expert")
-    my_index = lax.axis_index("expert")
-    per_kv = QUERY_HEADS // KEY_VALUE_HEADS
     kv_width = KEY_VALUE_HEADS * HEAD_SIZE
-    q_width = QUERY_HEADS * HEAD_SIZE
-    score_scale = 1.0 / math.sqrt(HEAD_SIZE)
-    group_tokens = token_count * group_size
+    group_tokens = token_count * lax.axis_size("expert")
     pack = pack_weights(w_router, norm_attn, norm_moe, w_query, key_projection, value_projection)
-    x_all, c_all, gw, uw, dw, pack, wo, kv_all, q_rot, attended, lse, middle = front(
+    x_all, c_all, gw, uw, dw, pack, wo, kv_all, q_rot, attended, lse, middle, pay = front(
         lengths,
         seq_order,
         tokens,
@@ -1123,141 +1785,36 @@
     grad_row, weighted, gate_grad, up_grad, down_grad = moe(
         x_all.reshape(group_tokens, width + 128), c_all.reshape(group_tokens, width), gw, uw, dw
     )
-    c_k = q_width
-    c_v = c_k + kv_width
-    c_s = c_v + kv_width
-    router_w = pack[:, c_s : c_s + n_experts]
-    gain_one = pack[:, c_s + n_experts].astype(F32)
-    gain_two = pack[:, c_s + n_experts + 1].astype(F32)
-    seq_lens, seq_ends = seq_layout(lengths, seq_order)
-    my_stream = lax.broadcasted_iota(jnp.int32, (token_count,), 0) * group_size + my_index
-    query_seq, query_rel = seq_place(my_stream, seq_lens, seq_ends)
-    all_rows = lax.broadcasted_iota(jnp.int32, (group_tokens,), 0)
-    key_stream = all_rows % token_count * group_size + all_rows // token_count
-    key_seq = seq_place(key_stream, seq_lens, seq_ends)[0]
-    cosine_table, sine_table = rope_tables(query_rel, HEAD_SIZE // 2)
-    inputs_float = tokens.astype(F32)
-    inv_one = rms_scale(inputs_float)
-    unit_one = inputs_float * inv_one
-    normed_one = (unit_one * gain_one).astype(BF)
-    rotated_queries = q_rot.transpose(1, 0, 2).reshape(
-        token_count, KEY_VALUE_HEADS, per_kv, HEAD_SIZE
-    )
-    gathered = kv_all.reshape(group_tokens, 2 * kv_width)
-    log_total = (
-        lse[..., 0]
-        .reshape(KEY_VALUE_HEADS, token_count // TILE, per_kv, TILE)
-        .transpose(0, 2, 1, 3)
-        .reshape(KEY_VALUE_HEADS, per_kv, token_count)
-        / LOG2E
-    )
-    attended_low = attended.astype(BF)
-    attended = attended.reshape(token_count, KEY_VALUE_HEADS, per_kv, HEAD_SIZE)
-    inv_two = rms_scale(middle)
-    unit_two = middle * inv_two
-    own = lax.dynamic_slice_in_dim(x_all, my_index, 1, 0)[0]
-    normed_two = own[:, :width]
-    ext = own[:, width:].astype(F32)
-    gates = ext[:, :n_experts] + ext[:, 32 : 32 + n_experts] + ext[:, 64 : 64 + n_experts]
-
-    row_sum = lax.psum_scatter(grad_row, "expert", scatter_dimension=0, tiled=True)
-    row_sum_grad = row_sum[:, :width]
-    ext = row_sum[:, width:].astype(F32)
-    grad_gates = ext[:, :n_experts] + ext[:, 32 : 32 + n_experts]
-    output = (
-        middle + lax.psum_scatter(weighted, "expert", scatter_dimension=0, tiled=True).astype(F32)
-    ).astype(BF)
-
-    grad_out = cotangent.astype(F32)
-    grad_logits = (
-        gates * (grad_gates - jnp.sum(gates * grad_gates, axis=1, keepdims=True))
-    ).astype(BF)
-    router_grad = dot_tn(normed_two, grad_logits)
-    grad_normed_two = dot_nt(grad_logits, router_w) + row_sum_grad.astype(F32)
-    gain_two_grad, grad_middle = norm_backward(grad_normed_two, unit_two, inv_two, gain_two)
-    grad_middle = grad_out + grad_middle
-    grad_mixed = grad_middle.astype(BF)
-    out_grad = dot_tn(attended_low, grad_mixed)
-    head_gradient = (
-        dot_nt(grad_mixed, wo).astype(BF).reshape(token_count, KEY_VALUE_HEADS, per_kv, HEAD_SIZE)
-    )
-    row_dot = jnp.transpose(jnp.sum(head_gradient.astype(F32) * attended, axis=-1), (1, 2, 0))
-    key_portion = gathered[:, :kv_width].reshape(-1, KEY_VALUE_HEADS, HEAD_SIZE)
-    value_portion = gathered[:, kv_width:].reshape(-1, KEY_VALUE_HEADS, HEAD_SIZE)
-    scores = block_scores(
-        rotated_queries, key_portion, query_seq, my_stream, key_seq, key_stream, score_scale
-    )
-    chances = jnp.exp(scores - log_total[..., None])
-    grad_chances = jnp.einsum(
-        "tkrd,skd->krts", head_gradient, value_portion, preferred_element_type=F32
-    )
-    grad_scores = (chances * (grad_chances - row_dot[..., None])).astype(BF)
-    query_grad = (
-        jnp.einsum("krts,skd->tkrd", grad_scores, key_portion, preferred_element_type=F32)
-        * score_scale
-    )
-    key_terms = (
-        jnp.einsum("krts,tkrd->skd", grad_scores, rotated_queries, preferred_element_type=F32)
-        * score_scale
-    )
-    value_terms = jnp.einsum(
-        "krts,tkrd->skd", chances.astype(BF), head_gradient, preferred_element_type=F32
-    )
-    kv_terms = jnp.concatenate(
-        [
-            key_terms.reshape(group_tokens, kv_width).astype(BF),
-            value_terms.reshape(group_tokens, kv_width).astype(BF),
-        ],
-        axis=1,
-    )
-    kv_mine = lax.psum_scatter(kv_terms, "expert", scatter_dimension=0, tiled=True)
-    grad_query_pre = (
-        reverse_rotation(
-            query_grad.reshape(token_count, QUERY_HEADS, HEAD_SIZE), cosine_table, sine_table
-        )
-        .reshape(token_count, q_width)
-        .astype(BF)
-    )
-    grad_key_pre = (
-        reverse_rotation(
-            kv_mine[:, :kv_width].astype(F32).reshape(token_count, KEY_VALUE_HEADS, HEAD_SIZE),
-            cosine_table,
-            sine_table,
-        )
-        .reshape(token_count, kv_width)
-        .astype(BF)
-    )
-    grad_qkv = jnp.concatenate([grad_query_pre, grad_key_pre, kv_mine[:, kv_width:]], axis=1)
-    grad_normed_one = dot_nt(grad_qkv, pack[:, :c_s])
-    qkv_grad = dot_tn(normed_one, grad_qkv)
-    gain_one_grad, grad_input = norm_backward(grad_normed_one, unit_one, inv_one, gain_one)
-    tokens_grad = (grad_middle + grad_input).astype(BF)
-    small_grad = jnp.concatenate(
-        [
-            router_grad,
-            gain_one_grad[:, None],
-            gain_two_grad[:, None],
-            jnp.zeros((width, 128 - n_experts - 2), F32),
-        ],
-        axis=1,
-    )
-    pack_grad = jnp.concatenate(
-        [qkv_grad.astype(BF), small_grad.astype(BF), out_grad.astype(BF)], axis=1
-    )
-    mine = lax.psum_scatter(pack_grad, ("dp", "expert"), scatter_dimension=0, tiled=True)
-    mine = mine.astype(F32)
     gate_mine, up_mine, down_mine = (
         lax.psum_scatter(grad, "dp", scatter_dimension=0, tiled=True).astype(F32)[None]
         for grad in (gate_grad, up_grad, down_grad)
     )
+    output, tokens_grad, query_mine, mine, out_mine = back(
+        lengths,
+        seq_order,
+        grad_row,
+        weighted,
+        tokens,
+        q_rot,
+        attended,
+        lse,
+        middle,
+        cotangent,
+        kv_all,
+        pay,
+        pack,
+        wo,
+        n_experts,
+    )
+    c_s = 2 * kv_width
     return (
         output,
         tokens_grad,
         mine[:, c_s + n_experts],
-        mine[:, :c_k],
-        mine[:, c_k:c_v],
-        mine[:, c_v:c_s],
-        mine[:, c_s + 128 :],
+        query_mine,
+        mine[:, :kv_width],
+        mine[:, kv_width:c_s],
+        out_mine,
         mine[:, c_s + n_experts + 1],
         mine[:, c_s : c_s + n_experts],
         gate_mine,

time: 788 us -> 442 us (0.56)
  waiting for transfers between devices: 383 us -> 1.4 us
  Pallas kernels: 225 us -> 402 us
  matrix products: 83.5 us -> 0 us
  local copies, waits for them, and re-layouts: 45.8 us -> 13.1 us
  other arithmetic: 25.5 us -> 6.72 us
    reduce_scatter x4 -> x0, waiting for transfers between devices: 267 us -> none  [the longest x1 149 us: on_device_fast(): lax.psum_scatter(pack_grad, ('dp', 'expert'), scatter_dimension=0, tiled=...]
    pallas_call x0 -> x1, Pallas kernels: none -> 168 us  [back(): pl.pallas_call(functools.partial(back_kernel, n_experts), in_specs=[smem,...]
    reduce_scatter x3, waiting for transfers between devices: 114 us -> 0.01 us  [on_device_fast(): lax.psum_scatter(grad, 'dp', scatter_dimension=0, tiled=True).astype(F32)]
    dot_general x11 -> x0, matrix products: 83.5 us -> none  [the longest x1 18.3 us: on_device_fast(): jnp.einsum('tkrd,skd->krts', head_gradient, value_portion, preferred_elem...]
    concatenate x1 -> x0, local copies, waits for them, and re-layouts: 17.5 us -> none  [on_device_fast(): jnp.concatenate([qkv_grad.astype(BF), small_grad.astype(BF), out_grad.ast...]
    pallas_call x1, Pallas kernels: 169 us -> 178 us  [front(): pl.pallas_call(functools.partial(front_kernel, n_experts), in_specs=[smem...]
  transfers between devices with their start and end apart: 7 -> 3, of which waited for: 7 -> 0; matrix products, arithmetic and copies ran while one was open for 11% -> 2% of each run, Pallas kernels for 0% -> 38%
where the time goes in v3:
time: 442 us; the launch traced here: 438 us
  Pallas kernels  402 us (91%)
  between operations  14 us (3%)
  local copies, waits for them, and re-layouts  13.1 us (3%)
  other arithmetic  6.72 us (2%)
    pallas_call x1, Pallas kernels, front(): pl.pallas_call(functools.partial(front_kernel, n_experts), in_specs=[smem...  178 us
    pallas_call x1, Pallas kernels, back(): pl.pallas_call(functools.partial(back_kernel, n_experts), in_specs=[smem,...  168 us
    pallas_call x1, Pallas kernels, moe(): pl.pallas_call(moe_kernel, grid=(rows // block,), in_specs=[moving(width...  56.4 us
  transfers between devices with their start and end apart: 3, of which 0 were waited for; matrix products, arithmetic and copies ran while one was open for 2% of the time, Pallas kernels for 38%

profile of v3, /device:TPU:0, one launch (start us, length us, event | category | flops | bytes accessed | tf_op | source)
XLA Modules:
  0.0 437.5 jit_solution(5242460564641405238)
XLA Ops:
  7.2 0.0 reduce-scatter.6.cloned.1.call-start
  7.2 0.8 copy.33
  8.0 0.8 copy.34
  8.7 0.8 copy.32
  9.5 1.5 copy.35.routes_ref
  11.0 1.7 concatenate.3.pack_ref
  12.7 177.9 %shard_map.238 = (bf16[8,256,1664]{2,1,0:T(8,128)(2,1)}, bf16[8,256,1536]{2,1,0:T(8,128)(2,1)}, bf16[1536,768]{1,0:T(8,128)(2,1)}, bf16[1536,768]{1,0:T(8,128)(2...) custom-call(s32[1,4]{1,0:T(1,128)} %lens_ref.3, ...), custom_call_target="tpu_custom_call" | custom-call | tf_op jit(solution)/shard_map/pallas_call | solution.py:922
  190.6 56.4 %shard_map.239 = (bf16[2048,1664]{1,0:T(8,128)(2,1)}, bf16[2048,1536]{1,0:T(8,128)(2,1)}, bf16[1536,768]{1,0:T(8,128)(2,1)}, bf16[1536,768]{1,0:T(8,128)(2,1)}, bf16[768,1536]{1,0:T(8,128)(2,1)}) custom-call(bf16[2048,1664]{1,0:T(8,128)(2,1)} %bitcast.25, bf16[2048,1536]{1,0:T(8,128)(2,1)} %bitcast.27, bf16[1536,768]{1,0:T(8,128)(2,1)} %get-tuple-element.37.gw, ...), custom_call_target="tpu_custom_call" | custom-call | flops 43486543872 | bytes 39321600 | tf_op jit(solution)/shard_map/pallas_call | solution.py:1029
  247.1 0.0 reduce-scatter.6.cloned.1.call-update
  247.1 0.0 reduce-scatter.8.cloned.1.call-start
  247.2 0.7 reduce-scatter.8.cloned.1.call-update
  247.9 0.0 reduce-scatter.4.cloned.1.call-start
  247.9 0.7 reduce-scatter.4.cloned.1.call-update
  248.6 167.9 %shard_map.240 = (bf16[256,1536]{1,0:T(8,128)(2,1)}, bf16[256,1536]{1,0:T(8,128)(2,1)}, f32[48,1536]{1,0:T(8,128)}, f32[48,640]{1,0:T(8,128)}, f32[48,1536]{1,0:T(8,128)}) custom-call(s32[1,4]{1,0:T(1,128)} %lens_ref.3, s32[1,4]{1,0:T(1,128)} %order_ref.3, bf16[4,2,256,1664]{3,2,1,0:T(8,128)(2,1)} %bitcast.29, bf16[4,2,256,1536]{3,2,1,0:T(8,128)(2,1)} %bitcast.30, ...), custom_call_target="tpu_custom_call" | custom-call | flops 149999992832 | bytes 50000000 | tf_op jit(solution)/shard_map/pallas_call | solution.py:1674
  416.5 0.7 slice.19
  417.2 0.7 copy.36
  417.9 1.5 slice_reduce_fusion
  419.4 1.5 fusion
  420.9 0.0 copy-start.1
  420.9 0.0 reduce-scatter.6.cloned.1.call-done
  420.9 2.2 bitcast_convert_fusion.1
  423.1 0.0 copy-start
  423.1 0.0 reduce-scatter.8.cloned.1.call-done
  423.1 2.3 bitcast_convert_fusion
  425.4 0.0 copy-start.3
  425.4 0.0 copy-start.2
  425.4 0.0 reduce-scatter.4.cloned.1.call-done
  425.4 2.2 bitcast_convert_fusion.2
  427.6 0.0 copy-done.1
  427.6 0.9 copy.41
  428.5 0.0 copy-done
  428.5 0.9 copy.42
  429.4 0.0 copy-done.3
  429.4 0.7 copy.43
  430.1 0.0 copy-done.2
  430.1 0.7 copy.44
  (1 shorter events, 0.0 us)
Async XLA Ops:
  7.2 413.7 %reduce-scatter.6.cloned.1.call-start = ((), (), s32[]{:S(2)}) async-start(), calls=%async_computation.4 | async-start | bytes 2949120 | tf_op jit(solution)/shard_map/reduce_scatter | solution.py:1789
  247.1 176.0 %reduce-scatter.8.cloned.1.call-start = ((), (), s32[]{:S(2)}) async-start(), calls=%async_computation.5 | async-start | bytes 2949120 | tf_op jit(solution)/shard_map/reduce_scatter | solution.py:1789
  247.9 177.5 %reduce-scatter.4.cloned.1.call-start = ((), (), s32[]{:S(2)}) async-start(), calls=%async_computation.3 | async-start | bytes 2949120 | tf_op jit(solution)/shard_map/reduce_scatter | solution.py:1789
  420.9 6.7 %copy-start.1 = (bf16[256,1536]{1,0:T(8,128)(2,1)S(1)}, bf16[256,1536]{1,0:T(8,128)(2,1)}, u32[]{:S(2)}) copy-start(bf16[256,1536]{1,0:T(8,128)(2,1)} %get-tuple-element.98) | copy-start | bytes 2359300
  423.1 5.4 %copy-start = (bf16[256,1536]{1,0:T(8,128)(2,1)S(1)}, bf16[256,1536]{1,0:T(8,128)(2,1)}, u32[]{:S(2)}) copy-start(bf16[256,1536]{1,0:T(8,128)(2,1)} %get-tuple-element.99) | copy-start | bytes 2359300
  425.4 4.0 copy-start.3
  425.4 4.7 %copy-start.2 = (f32[48,1536]{1,0:T(8,128)S(1)}, f32[48,1536]{1,0:T(8,128)}, u32[]{:S(2)}) copy-start(f32[48,1536]{1,0:T(8,128)} %get-tuple-element.104) | copy-start | bytes 884740
Sparse Core Ops, SparseCore 0:
  247.2 47.4 reduce-scatter.5
  297.0 56.7 reduce-scatter.7
  356.1 53.6 reduce-scatter.3
